TPU v7x, 128 devices: a whole 4x4x4 slice. The times are simulated.
128 devices in a mesh: lon: 16 (over x_lo, z, core), lat: 8 (over x_hi, y).
Axes of the slice: x: 4 (x_hi: 2, x_lo: 2; x = x_hi * 2 + x_lo), y: 4, z: 4, core: 2. Of those that a mesh axis runs over, the one named last changes fastest.
Arguments:
- tokens: bfloat16 [384, 768, 512], P('lat', 'lon'), may hold values from -6 to 6
- valid: int32 [384, 768], P('lat', 'lon'), may hold values from 0 to 1, as said below
- w_qkv: bfloat16 [2, 512, 1536], replicated, may hold values from -1.5 to 1.5
- w_out: bfloat16 [2, 512, 512], replicated, may hold values from -0.25 to 0.25
- w_up: bfloat16 [2, 512, 2048], replicated, may hold values from -0.25 to 0.25
- w_down: bfloat16 [2, 2048, 512], replicated, may hold values from -0.125 to 0.125
Outputs:
- result: bfloat16 [384, 768, 512], P('lat', 'lon')
Inputs may be any that keep to these rules, and one draw needn't show every extreme that they name: In each band of 12 longitude columns starting at a multiple of 12, valid is 0 on the last p latitude rows of the grid and 1 elsewhere, p from 0 to 5; p = 5 in some band.
All inputs are finite; a program needn't handle non-finite values.
Results may differ from a plain program's by a relative error of at most 0.025.
Values may be sent and summed in bfloat16 or wider, within the bound.
A program may use at most 192 MiB of HBM per device.

v0:
```python
import jax
import jax.numpy as jnp
from jax import lax
from jax.sharding import PartitionSpec as P

HEADS = 16
WIN_H = 6
WIN_W = 12


def shifted(value, axis, steps):
    count = lax.axis_size(axis)
    pairs = [(source, (source + steps) % count) for source in range(count)]
    return lax.ppermute(value, axis, pairs)


def passed_along(block, axis, distance):
    devices = range(lax.axis_size(axis))
    route = [(i - distance, i) for i in devices if i - distance in devices]
    return lax.ppermute(block, axis, route)


def layer_norm(values):
    wide = values.astype(jnp.float32)
    center = wide - jnp.mean(wide, axis=-1, keepdims=True)
    spread = jnp.mean(center * center, axis=-1, keepdims=True)
    return center * lax.rsqrt(spread + 1e-05)


def to_windows(grid, win_h, win_w):
    height, width = (grid.shape[0], grid.shape[1])
    rest = grid.shape[2:]
    tiles = grid.reshape((height // win_h, win_h, width // win_w, win_w) + rest)
    tiles = jnp.moveaxis(tiles, 2, 1)
    return tiles.reshape((height // win_h * (width // win_w), win_h * win_w) + rest)


def from_windows(windows, height, width, win_h, win_w):
    rest = windows.shape[2:]
    tiles = windows.reshape((height // win_h, width // win_w, win_h, win_w) + rest)
    tiles = jnp.moveaxis(tiles, 1, 2)
    return tiles.reshape((height, width) + rest)


def attend(windows, keyok, region, w_qkv, w_out, w_up, w_down):
    count, length, width = windows.shape
    head_dim = width // HEADS
    normed = layer_norm(windows).astype(jnp.bfloat16).reshape(count * length, width)
    qkv = jnp.dot(normed, w_qkv, preferred_element_type=jnp.float32).astype(jnp.bfloat16)
    qkv = qkv.reshape(count, length, 3, HEADS, head_dim)
    query, keys, values = (qkv[:, :, 0], qkv[:, :, 1], qkv[:, :, 2])
    scores = jnp.einsum(
        "nqhd,nkhd->nhqk", query, keys, preferred_element_type=jnp.float32
    ) * head_dim ** (-0.5)
    itself = jnp.eye(length, dtype=bool)[None]
    allowed = (keyok[:, None, :] | itself) & (region[:, :, None] == region[:, None, :])
    scores = jnp.where(allowed[:, None], scores, -jnp.inf)
    largest = jnp.max(scores, axis=-1, keepdims=True)
    expo = jnp.exp(scores - largest)
    probs = (expo / jnp.sum(expo, axis=-1, keepdims=True)).astype(jnp.bfloat16)
    mixed = jnp.einsum("nhqk,nkhd->nqhd", probs, values, preferred_element_type=jnp.float32)
    mixed = mixed.astype(jnp.bfloat16).reshape(count * length, width)
    flat = windows.reshape(count * length, width).astype(jnp.float32)
    resid = (flat + jnp.dot(mixed, w_out, preferred_element_type=jnp.float32)).astype(jnp.bfloat16)
    normed_two = layer_norm(resid).astype(jnp.bfloat16)
    hidden = jax.nn.gelu(jnp.dot(normed_two, w_up, preferred_element_type=jnp.float32)).astype(
        jnp.bfloat16
    )
    output = resid.astype(jnp.float32) + jnp.dot(hidden, w_down, preferred_element_type=jnp.float32)
    return output.astype(jnp.bfloat16).reshape(count, length, width)


def run_frame(frame, flags, region, win_h, w_qkv, w_out, w_up, w_down):
    height, width = (frame.shape[0], frame.shape[1])
    output = attend(
        to_windows(frame, win_h, WIN_W),
        to_windows(flags, win_h, WIN_W),
        to_windows(region, win_h, WIN_W),
        w_qkv,
        w_out,
        w_up,
        w_down,
    )
    return from_windows(output, height, width, win_h, WIN_W)


def shards(tokens, valid, w_qkv, w_out, w_up, w_down):
    rows, cols, width = tokens.shape
    half_h = WIN_H // 2
    half_w = WIN_W // 2
    keyok = valid == 1
    flat_region = jnp.zeros((rows, cols), jnp.int32)
    first = run_frame(tokens, keyok, flat_region, WIN_H, w_qkv[0], w_out[0], w_up[0], w_down[0])
    mask = valid.astype(jnp.bfloat16)
    northmost = lax.axis_index("lat") == 0
    right, right_mask = shifted((first, mask), "lon", -1)
    extended = jnp.concatenate([first[:, half_w:], right[:, :half_w]], axis=1)
    ext_mask = jnp.concatenate([mask[:, half_w:], right_mask[:, :half_w]], axis=1)
    above, above_mask = passed_along((extended, ext_mask), "lat", 1)
    above = above[above.shape[0] - half_h :]
    above_mask = above_mask[above_mask.shape[0] - half_h :]
    frame = jnp.concatenate([above, extended[: rows - half_h]], axis=0)
    frame_ok = jnp.concatenate([above_mask, ext_mask[: rows - half_h]], axis=0) > 0.5
    top_rows = (jnp.arange(rows) < half_h)[:, None] & northmost
    region = jnp.broadcast_to(jnp.where(top_rows, 1, 0).astype(jnp.int32), (rows, cols))
    second = run_frame(frame, frame_ok, region, WIN_H, w_qkv[1], w_out[1], w_up[1], w_down[1])
    below = passed_along(second, "lat", -1)[:half_h]
    pole_in = extended[rows - half_h :]
    pole_ok = ext_mask[rows - half_h :] > 0.5
    pole_region = jnp.zeros((half_h, cols), jnp.int32)
    pole_out = run_frame(
        pole_in, pole_ok, pole_region, half_h, w_qkv[1], w_out[1], w_up[1], w_down[1]
    )
    southmost = lax.axis_index("lat") == lax.axis_size("lat") - 1
    below = jnp.where(southmost, pole_out, below)
    settled = jnp.concatenate([second[half_h:], below], axis=0)
    left = shifted(settled, "lon", 1)[:, cols - half_w :]
    result = jnp.concatenate([left, settled[:, : cols - half_w]], axis=1)
    return (result.astype(jnp.float32) * valid.astype(jnp.float32)[:, :, None]).astype(jnp.bfloat16)


def solution(mesh):
    return jax.shard_map(
        shards,
        mesh=mesh,
        in_specs=(P("lat", "lon", None), P("lat", "lon"), P(), P(), P(), P()),
        out_specs=P("lat", "lon", None),
        check_vma=False,
    )
```

profile of v0, /device:TPU:24, one launch (start us, length us, event | category | flops | bytes accessed | tf_op | source)
XLA Modules:
  0.0 571.3 jit_solution(12599516272081059892)
XLA Ops:
  0.0 1.4 fusion.172
  1.4 4.4 collective-permute-start.2
  6.6 5.3 reshape.274
  11.9 3.4 bitcast_reduce_fusion.2
  19.3 2.1 convert_element_type.186
  21.4 8.9 %convolution_convert_fusion.1 = bf16[2304,1536]{1,0:T(8,128)(2,1)} fusion(bf16[2304,512]{1,0:T(8,128)(2,1)} %convert_element_type.186, bf16[2,512,1536]{2,1,0:T(8,128)(2,1)} %param.8), kind=kOutput, calls=%fused_computation.30 | convolution fusion | flops 3627417600 | bytes 11010048 | tf_op jit(solution)/shard_map/dot_general | solution.py:49
  30.3 9.9 %copy.24 = bf16[2304,1536]{0,1:T(8,128)(2,1)} copy(bf16[2304,1536]{1,0:T(8,128)(2,1)} %convolution_convert_fusion.1) | data formatting | bytes 14155776 | tf_op jit(solution)/shard_map/convert_element_type | solution.py:49
  40.1 30.1 %reshape.257 = bf16[32,72,3,16,32]{1,0,4,3,2:T(8,128)(2,1)} reshape(bf16[2304,1536]{0,1:T(8,128)(2,1)} %copy.24) | data formatting | bytes 14155776 | tf_op jit(solution)/shard_map/reshape | solution.py:50
  70.2 9.2 %fusion.170 = (bf16[32,72,1,16,32]{1,0,4,3,2:T(8,128)(2,1)}, bf16[32,72,1,16,32]{1,0,4,3,2:T(8,128)(2,1)}, bf16[32,72,1,16,32]{1,0,4,3,2:T(8,128)(2,1)}) fusion(bf16[32,72,3,16,32]{1,0,4,3,2:T(8,128)(2,1)} %reshape.257), kind=kLoop, calls=%fused_computation.209 | loop fusion | bytes 14155776 | tf_op jit(solution)/shard_map/slice | solution.py:51
  79.5 19.0 %fusion.54 = f32[32,16,72,72]{2,3,1,0:T(8,128)} fusion(bf16[32,72,1,16,32]{1,0,4,3,2:T(8,128)(2,1)} %get-tuple-element.10, bf16[32,72,1,16,32]{1,0,4,3,2:T(8,128)(2,1)} %get-tuple-element.9), kind=kOutput, calls=%fused_computation.73 | convolution fusion | flops 169869312 | bytes 15335424 | tf_op jit(solution)/shard_map/nqhd,nkhd->nhqk/dot_general | solution.py:52
  99.0 6.9 %copy.22 = f32[8,4,6,12,512]{4,3,2,1,0:T(8,128)} copy(f32[8,4,6,12,512]{4,3,1,2,0:T(8,128)} %bitcast.144) | data formatting | bytes 9437184 | tf_op jit(solution)/shard_map/convert_element_type | solution.py:63
  105.8 6.7 %reshape.268 = f32[2304,512]{1,0:T(8,128)} reshape(f32[8,4,6,12,512]{4,3,2,1,0:T(8,128)} %copy.22) | data formatting | bytes 9437184 | tf_op jit(solution)/shard_map/convert_element_type | solution.py:63
  112.7 4.3 collective-permute-start.3
  118.6 2.6 compare_and_fusion
  121.1 22.2 %fusion.173 = (f32[32,16,72]{2,1,0:T(8,128)S(1)}, f32[32,16,72,72]{2,3,1,0:T(8,128)}) fusion(f32[32,16,72,72]{2,3,1,0:T(8,128)} %fusion.54, pred[32,72,72]{1,2,0:T(8,128)(4,1)S(1)} %get-tuple-element.17), kind=kOutput, calls=%fused_computation.212 | output fusion | flops 15925319 | bytes 21547008 | tf_op jit(solution)/shard_map/sub | solution.py:59
  143.3 14.9 %convert_bitcast_fusion.1 = bf16[32,72,16,32]{1,3,2,0:T(8,128)(2,1)} fusion(f32[32,16,72,72]{2,3,1,0:T(8,128)} %get-tuple-element.19, f32[32,16,72]{2,1,0:T(8,128)S(1)} %get-tuple-element.18, bf16[32,72,1,16,32]{1,0,4,3,2:T(8,128)(2,1)} %get-tuple-element.8), kind=kOutput, calls=%fused_computation.77 | convolution fusion | flops 176357376 | bytes 15482880 | tf_op jit(solution)/shard_map/nhqk,nkhd->nqhd/dot_general | solution.py:61
  158.2 6.9 %copy.30 = bf16[32,72,16,32]{1,0,3,2:T(8,128)(2,1)} copy(bf16[32,72,16,32]{1,3,2,0:T(8,128)(2,1)} %convert_bitcast_fusion.1) | data formatting | bytes 4718592 | tf_op jit(solution)/shard_map/convert_element_type | solution.py:62
  165.1 7.3 %reshape.259 = bf16[2304,512]{0,1:T(8,128)(2,1)S(1)} reshape(bf16[32,72,16,32]{1,0,3,2:T(8,128)(2,1)} %copy.30) | data formatting | bytes 4718592 | tf_op jit(solution)/shard_map/reshape | solution.py:62
  172.4 3.8 convert_reduce_fusion.1
  176.2 1.4 copy-done.2
  178.8 15.4 %fusion.45 = bf16[2304,512]{1,0:T(8,128)(2,1)} fusion(bf16[2304,512]{1,0:T(8,128)(2,1)} %copy-done.2, f32[2304]{0:T(1024)S(1)} %add_rsqrt_fusion.3, f32[2304]{0:T(1024)S(1)} %broadcast_multiply_fusion.3, bf16[2,2048,512]{2,1,0:T(8,128)(2,1)} %param.11, bf16[2,512,2048]{2,1,0:T(8,128)(2,1)} %param.10), kind=kOutput, calls=%fused_computation.63 | convolution fusion | flops 9714401280 | bytes 11290624 | tf_op jit(solution)/shard_map/dot_general | solution.py:69
  194.2 3.5 reshape_reshape.12
  197.7 2.1 copy.31
  199.8 4.9 reshape.260
  204.7 3.0 slice.131
  207.8 23.6 %collective-permute-done = bf16[48,48,512]{2,1,0:T(8,128)(2,1)S(1)} collective-permute-done((bf16[48,48,512]{2,1,0:T(8,128)(2,1)}, bf16[48,48,512]{2,1,0:T(8,128)(2,1)S(1)}, u32[]{:S(2)}, u32[]{:S(2)}) %collective-permute-start) | collective-permute-done | bytes 2359328 | tf_op jit(solution)/shard_map/ppermute | solution.py:14
  231.4 1.8 pad_maximum_fusion
  233.2 7.8 %collective-permute-start.1 = (bf16[48,48,512]{2,1,0:T(8,128)(2,1)}, bf16[48,48,512]{2,1,0:T(8,128)(2,1)}, u32[]{:S(2)}, u32[]{:S(2)}) collective-permute-start(bf16[48,48,512]{2,1,0:T(8,128)(2,1)} %pad_maximum_fusion), channel_id=1, source_target_pairs={{0,1},{1,2},{2,3},{3,4},{4,5},{5,6},{6,7},{8,9},{9,10},{10,11},{11... | collective-permute-start | bytes 7077896 | tf_op jit(solution)/shard_map/ppermute | solution.py:20
  244.3 45.6 %collective-permute-done.1 = bf16[48,48,512]{2,1,0:T(8,128)(2,1)} collective-permute-done((bf16[48,48,512]{2,1,0:T(8,128)(2,1)}, bf16[48,48,512]{2,1,0:T(8,128)(2,1)}, u32[]{:S(2)}, u32[]{:S(2)}) %collective-permute-start.1) | collective-permute-done | bytes 2359328 | tf_op jit(solution)/shard_map/ppermute | solution.py:20
  290.9 2.4 maximum_convert_fusion
  293.3 6.7 %reshape.275 = f32[8,6,4,12,512]{4,3,2,1,0:T(8,128)} reshape(f32[48,48,512]{2,1,0:T(8,128)} %maximum_convert_fusion) | data formatting | bytes 9437184 | tf_op jit(solution)/shard_map/convert_element_type | solution.py:63
  300.0 3.4 bitcast_reduce_fusion.1
  307.4 2.1 convert_element_type.202
  309.6 8.9 %convolution_convert_fusion = bf16[2304,1536]{1,0:T(8,128)(2,1)} fusion(bf16[2304,512]{1,0:T(8,128)(2,1)} %convert_element_type.202, bf16[2,512,1536]{2,1,0:T(8,128)(2,1)} %param.8), kind=kOutput, calls=%fused_computation.29 | convolution fusion | flops 3627417600 | bytes 11010048 | tf_op jit(solution)/shard_map/dot_general | solution.py:49
  318.4 9.9 %copy.34 = bf16[2304,1536]{0,1:T(8,128)(2,1)} copy(bf16[2304,1536]{1,0:T(8,128)(2,1)} %convolution_convert_fusion) | data formatting | bytes 14155776 | tf_op jit(solution)/shard_map/convert_element_type | solution.py:49
  328.3 30.2 %reshape.261 = bf16[32,72,3,16,32]{1,0,4,3,2:T(8,128)(2,1)} reshape(bf16[2304,1536]{0,1:T(8,128)(2,1)} %copy.34) | data formatting | bytes 14155776 | tf_op jit(solution)/shard_map/reshape | solution.py:50
  358.6 9.2 %fusion.169 = (bf16[32,72,1,16,32]{1,0,4,3,2:T(8,128)(2,1)}, bf16[32,72,1,16,32]{1,0,4,3,2:T(8,128)(2,1)}, bf16[32,72,1,16,32]{1,0,4,3,2:T(8,128)(2,1)}) fusion(bf16[32,72,3,16,32]{1,0,4,3,2:T(8,128)(2,1)} %reshape.261), kind=kLoop, calls=%fused_computation.208 | loop fusion | bytes 14155776 | tf_op jit(solution)/shard_map/slice | solution.py:51
  368.1 3.4 copy.32
  371.4 7.1 %reshape.269 = f32[2304,512]{1,0:T(8,128)} reshape(f32[8,4,6,12,512]{4,3,2,1,0:T(8,128)} %copy.32) | data formatting | bytes 9437184 | tf_op jit(solution)/shard_map/convert_element_type | solution.py:63
  378.6 19.0 %fusion.53 = f32[32,16,72,72]{2,3,1,0:T(8,128)} fusion(bf16[32,72,1,16,32]{1,0,4,3,2:T(8,128)(2,1)} %get-tuple-element.7, bf16[32,72,1,16,32]{1,0,4,3,2:T(8,128)(2,1)} %get-tuple-element.6), kind=kOutput, calls=%fused_computation.69 | convolution fusion | flops 169869312 | bytes 15335424 | tf_op jit(solution)/shard_map/nqhd,nkhd->nhqk/dot_general | solution.py:52
  397.6 22.4 %fusion.180 = (f32[32,16,72]{2,1,0:T(8,128)S(1)}, f32[32,16,72,72]{2,3,1,0:T(8,128)}) fusion(f32[32,16,72,72]{2,3,1,0:T(8,128)} %fusion.53, pred[32,72,72]{1,2,0:T(8,128)(4,1)S(1)} %copy-done.8), kind=kOutput, calls=%fused_computation.215 | output fusion | flops 15925319 | bytes 21547008 | tf_op jit(solution)/shard_map/sub | solution.py:59
  419.9 14.9 %convert_bitcast_fusion = bf16[32,72,16,32]{1,3,2,0:T(8,128)(2,1)} fusion(f32[32,16,72,72]{2,3,1,0:T(8,128)} %get-tuple-element.27, f32[32,16,72]{2,1,0:T(8,128)S(1)} %get-tuple-element.26, bf16[32,72,1,16,32]{1,0,4,3,2:T(8,128)(2,1)} %get-tuple-element.5), kind=kOutput, calls=%fused_computation.76 | convolution fusion | flops 176357376 | bytes 15482880 | tf_op jit(solution)/shard_map/nhqk,nkhd->nqhd/dot_general | solution.py:61
  434.8 6.9 %copy.40 = bf16[32,72,16,32]{1,0,3,2:T(8,128)(2,1)} copy(bf16[32,72,16,32]{1,3,2,0:T(8,128)(2,1)} %convert_bitcast_fusion) | data formatting | bytes 4718592 | tf_op jit(solution)/shard_map/convert_element_type | solution.py:62
  441.7 7.3 %reshape.262 = bf16[2304,512]{0,1:T(8,128)(2,1)S(1)} reshape(bf16[32,72,16,32]{1,0,3,2:T(8,128)(2,1)} %copy.40) | data formatting | bytes 4718592 | tf_op jit(solution)/shard_map/reshape | solution.py:62
  449.0 3.8 convert_reduce_fusion
  452.9 1.4 copy-done.3
  455.4 15.5 %fusion.46 = bf16[2304,512]{1,0:T(8,128)(2,1)} fusion(bf16[2304,512]{1,0:T(8,128)(2,1)} %copy-done.3, f32[2304]{0:T(1024)S(1)} %add_rsqrt_fusion.2, f32[2304]{0:T(1024)S(1)} %broadcast_multiply_fusion.2, bf16[2,2048,512]{2,1,0:T(8,128)(2,1)} %param.11, bf16[2,512,2048]{2,1,0:T(8,128)(2,1)} %param.10), kind=kOutput, calls=%fused_computation.64 | convolution fusion | flops 9714401280 | bytes 11290624 | tf_op jit(solution)/shard_map/dot_general | solution.py:69
  471.0 3.5 reshape_reshape.13
  474.4 2.1 copy.41
  476.5 3.7 reshape.263
  480.2 1.9 collective-permute-start.4
  482.2 1.8 convolution_convert_fusion.2
  484.0 2.3 reshape.264
  486.3 2.6 fusion.171
  488.9 2.4 copy.60
  491.4 1.4 copy.61
  493.4 2.9 fusion.174
  496.2 2.7 fusion.96
  499.0 2.5 copy.49
  501.5 1.6 reshape.266
  505.3 3.4 fusion.114
  509.0 27.8 %collective-permute-done.4 = bf16[48,48,512]{2,1,0:T(8,128)(2,1)} collective-permute-done((bf16[48,48,512]{2,1,0:T(8,128)(2,1)S(1)}, bf16[48,48,512]{2,1,0:T(8,128)(2,1)}, u32[]{:S(2)}, u32[]{:S(2)}) %collective-permute-start.4) | collective-permute-done | bytes 2359328 | tf_op jit(solution)/shard_map/ppermute | solution.py:20
  538.3 30.2 %collective-permute-done.5 = bf16[48,48,512]{2,1,0:T(8,128)(2,1)S(1)} collective-permute-done((bf16[48,48,512]{2,1,0:T(8,128)(2,1)S(1)}, bf16[48,48,512]{2,1,0:T(8,128)(2,1)S(1)}, u32[]{:S(2)}, u32[]{:S(2)}) %collective-permute-start.5) | collective-permute-done | bytes 2359328 | tf_op jit(solution)/shard_map/ppermute | solution.py:14
  568.5 2.3 multiply_convert_fusion.2
  (94 shorter events, 22.2 us)
Async XLA Ops:
  1.4 111.1 %collective-permute-start.2 = (bf16[48,48]{1,0:T(8,128)(2,1)S(1)}, bf16[48,48]{1,0:T(8,128)(2,1)S(1)}, u32[]{:S(2)}, u32[]{:S(2)}) collective-permute-start(bf16[48,48]{1,0:T(8,128)(2,1)S(1)} %get-tuple-element.15), channel_id=1, source_target_pairs={{0,120},{8,0},{16,8},{24,16},{32,24},{40,32},{48,40},{56,48},{64,5... | collective-permute-start | bytes 13832 | tf_op jit(solution)/shard_map/ppermute | solution.py:14
  11.9 4.6 copy-start
  112.7 5.7 collective-permute-start.3
  165.1 7.3 %copy-start.4 = (bf16[2,512,512]{2,1,0:T(8,128)(2,1)S(1)}, bf16[2,512,512]{2,1,0:T(8,128)(2,1)}, u32[]{:S(2)}) copy-start(bf16[2,512,512]{2,1,0:T(8,128)(2,1)} %param.9) | copy-start | bytes 3145732
  176.2 1.4 copy-start.2
  204.7 26.7 %collective-permute-start = (bf16[48,48,512]{2,1,0:T(8,128)(2,1)}, bf16[48,48,512]{2,1,0:T(8,128)(2,1)S(1)}, u32[]{:S(2)}, u32[]{:S(2)}) collective-permute-start(bf16[48,48,512]{2,1,0:T(8,128)(2,1)} %reshape.260), channel_id=1, source_target_pairs={{0,120},{8,0},{16,8},{24,16},{32,24},{40,32},{48,40},{56,48},{64,5... | collective-permute-start | bytes 7077896 | tf_op jit(solution)/shard_map/ppermute | solution.py:14
  233.2 56.8 %collective-permute-start.1 = (bf16[48,48,512]{2,1,0:T(8,128)(2,1)}, bf16[48,48,512]{2,1,0:T(8,128)(2,1)}, u32[]{:S(2)}, u32[]{:S(2)}) collective-permute-start(bf16[48,48,512]{2,1,0:T(8,128)(2,1)} %pad_maximum_fusion), channel_id=1, source_target_pairs={{0,1},{1,2},{2,3},{3,4},{4,5},{5,6},{6,7},{8,9},{9,10},{10,11},{11... | collective-permute-start | bytes 7077896 | tf_op jit(solution)/shard_map/ppermute | solution.py:20
  300.0 4.6 copy-start.1
  328.3 39.5 %slice-start = ((s8[6291456]{0:T(1024)(128)(4,1)}), s8[2097152]{0:T(1024)(128)(4,1)S(1)}, s32[]{:S(2)}) async-start(s8[6291456]{0:T(1024)(128)(4,1)} %bitcast.145), calls=%async_computation | async-start | bytes 4194304
  358.5 9.5 %slice-start.1 = ((s8[6291456]{0:T(1024)(128)(4,1)}), s8[4194304]{0:T(1024)(128)(4,1)S(1)}, s32[]{:S(2)}) async-start(s8[6291456]{0:T(1024)(128)(4,1)} %bitcast.145), calls=%async_computation.1 | async-start | bytes 8388608
  378.5 19.0 %copy-start.8 = (pred[32,72,72]{1,2,0:T(8,128)(4,1)S(1)}, pred[32,72,72]{1,2,0:T(8,128)(4,1)}, u32[]{:S(2)}) copy-start(pred[32,72,72]{1,2,0:T(8,128)(4,1)} %get-tuple-element.16) | copy-start | bytes 497668
  441.7 7.3 %copy-start.5 = (bf16[2,512,512]{2,1,0:T(8,128)(2,1)S(1)}, bf16[2,512,512]{2,1,0:T(8,128)(2,1)}, u32[]{:S(2)}) copy-start(bf16[2,512,512]{2,1,0:T(8,128)(2,1)} %param.9) | copy-start | bytes 3145732
  452.9 1.4 copy-start.3
  476.5 5.6 copy-start.9
  480.2 56.6 %collective-permute-start.4 = (bf16[48,48,512]{2,1,0:T(8,128)(2,1)S(1)}, bf16[48,48,512]{2,1,0:T(8,128)(2,1)}, u32[]{:S(2)}, u32[]{:S(2)}) collective-permute-start(bf16[48,48,512]{2,1,0:T(8,128)(2,1)S(1)} %reshape.263), channel_id=1, source_target_pairs={{1,0},{2,1},{3,2},{4,3},{5,4},{6,5},{7,6},{9,8},{10,9},{11,10},{12... | collective-permute-start | bytes 7077896 | tf_op jit(solution)/shard_map/ppermute | solution.py:20
  496.2 6.8 %copy-start.6 = (bf16[2,512,512]{2,1,0:T(8,128)(2,1)S(1)}, bf16[2,512,512]{2,1,0:T(8,128)(2,1)}, u32[]{:S(2)}) copy-start(bf16[2,512,512]{2,1,0:T(8,128)(2,1)} %param.9) | copy-start | bytes 3145732
  504.4 0.7 copy-start.7
  537.7 30.8 %copy-start.10 = (f32[48,48]{1,0:T(8,128)S(1)}, f32[48,48]{1,0:T(8,128)}, u32[]{:S(2)}) copy-start(f32[48,48]{1,0:T(8,128)} %get-tuple-element.14) | copy-start | bytes 27652
  538.0 30.4 %collective-permute-start.5 = (bf16[48,48,512]{2,1,0:T(8,128)(2,1)S(1)}, bf16[48,48,512]{2,1,0:T(8,128)(2,1)S(1)}, u32[]{:S(2)}, u32[]{:S(2)}) collective-permute-start(bf16[48,48,512]{2,1,0:T(8,128)(2,1)S(1)} %pad_maximum_fusion.1), channel_id=1, source_target_pairs={{0,8},{8,16},{16,24},{24,32},{32,40},{40,48},{48,56},{56,64},{64,7... | collective-permute-start | bytes 7077896 | tf_op jit(solution)/shard_map/ppermute | solution.py:14
where the time goes:
time: 580 us; the launch traced here: 571 us
  local copies, waits for them, and re-layouts  214 us (37%)
  matrix products  136 us (23%)
  waiting for transfers between devices  129 us (22%)
  other arithmetic  73 us (13%)
  starting transfers between devices  18.5 us (3%)
    ppermute x3, waiting for transfers between devices, passed_along(): return lax.ppermute(block, axis, route)  74.7 us
    reshape x3, local copies, waits for them, and re-layouts, attend(): qkv = qkv.reshape(count, length, 3, HEADS, head_dim)  62.7 us
    ppermute x3, waiting for transfers between devices, shifted(): return lax.ppermute(value, axis, pairs)  53.8 us
    sub x2, other arithmetic, attend(): expo = jnp.exp(scores - largest)  44.5 us
    dot_general x2, matrix products, attend(): jnp.einsum('nqhd,nkhd->nhqk', query, keys, preferred_element_type=jnp.flo...  38 us
    convert_element_type x9, local copies, waits for them, and re-layouts, attend(): flat = windows.reshape(count * length, width).astype(jnp.float32)  36.9 us
    dot_general x3, matrix products, attend(): jnp.dot(hidden, w_down, preferred_element_type=jnp.float32)  34.3 us
    dot_general x3, matrix products, attend(): jnp.einsum('nhqk,nkhd->nqhd', probs, values, preferred_element_type=jnp.f...  32.5 us
  transfers between devices with their start and end apart: 6, of which 5 were waited for; matrix products, arithmetic and copies ran while one was open for 24% of the time, Pallas kernels for 0%

commit v1 on v0

v1 whole, which is shorter than its diff:
```python
import jax
import jax.numpy as jnp
import numpy as np
from jax import lax
from jax.experimental import pallas as pl
from jax.experimental.pallas import tpu as pltpu
from jax.sharding import PartitionSpec as P

HEADS = 16
WIN_H = 6
WIN_W = 12
TOK = WIN_H * WIN_W
PAD = 80
EXT = 64
HALO = 16
MESH = pl.DeviceIdType.MESH
BF = jnp.bfloat16
F32 = jnp.float32


def to_window_order(rows, cols, offset, win_h):
    take = np.zeros((rows * 48, rows * cols), np.float32)
    t = 0
    for band in range(rows // win_h):
        for j in range(4):
            for r in range(win_h):
                for c in range(WIN_W):
                    take[t, (band * win_h + r) * cols + offset + j * WIN_W + c] = 1
                    t += 1
    return take


def head_sets():
    head = np.arange(256) // 32
    return np.stack([head // 3 == i for i in range(3)] + [head % 3 == j for j in range(3)])[:, None, :]


def layer_norm(wide):
    center = wide - jnp.mean(wide, axis=-1, keepdims=True)
    spread = jnp.mean(center * center, axis=-1, keepdims=True)
    return (center * lax.rsqrt(spread + 1e-05)).astype(BF)


def gelu(x):
    half = 0.5 * x
    return half + half * jnp.tanh(x * (0.7978845608028654 + 0.035677408136300125 * (x * x)))


def half_heads(q, k, v, sets, allow):
    by_key = jnp.concatenate([k * sets[i] for i in range(3)], 0)
    by_query = jnp.concatenate([q * sets[3 + j] for j in range(3)], 0)
    scores = lax.dot_general(by_key, by_query, (((1,), (1,)), ((), ())), preferred_element_type=F32)
    parts = []
    for i in range(3):
        part = scores[PAD * i : PAD * i + TOK]
        if allow is not None:
            part = jnp.where(allow, part, -jnp.inf)
        largest = jnp.max(part, axis=0, keepdims=True)
        expo = jnp.exp2((part - largest) * (1.4426950408889634 * 32**-0.5))
        total = jnp.sum(expo, axis=0, keepdims=True)
        parts += [expo * (1.0 / total), jnp.zeros((PAD - TOK, 3 * PAD), F32)]
    probs = jnp.concatenate(parts, 0).astype(BF)
    by_value = jnp.concatenate([v * sets[i] for i in range(3)], 0)
    mixed = lax.dot_general(probs, by_value, (((0,), (0,)), ((), ())), preferred_element_type=F32)
    pick = [sets[3 + j].astype(F32) for j in range(3)]
    return (
        mixed[:TOK] * pick[0] + mixed[PAD : PAD + TOK] * pick[1] + mixed[2 * PAD : 2 * PAD + TOK] * pick[2]
    )


def attention(qkv, mixed, sets_ref, count, flags=None, halves=False):
    sets = [sets_ref[i] for i in range(6)]
    key = lax.broadcasted_iota(jnp.int32, (TOK, 3 * PAD), 0)
    lane = lax.broadcasted_iota(jnp.int32, (TOK, 3 * PAD), 1)
    query = lane - PAD * (lane >= PAD).astype(jnp.int32) - PAD * (lane >= 2 * PAD).astype(jnp.int32)
    for pair in range(count // 2):
        for g in range(2):
            both = []
            for w in (2 * pair, 2 * pair + 1):
                allow = None
                if flags is not None:
                    allow = flags[w][:, 0:1] > 0.5
                    if halves:
                        allow = allow & ((key < TOK // 2) == (query < TOK // 2))
                    allow = allow | (key == query)
                q = qkv[w, :, 256 * g : 256 * g + 256]
                k = qkv[w, :, 512 + 256 * g : 768 + 256 * g]
                v = qkv[w, :, 1024 + 256 * g : 1280 + 256 * g]
                both.append(half_heads(q, k, v, sets, allow))
            mixed[2 * TOK * pair : 2 * TOK * pair + 2 * TOK, 256 * g : 256 * g + 256] = jnp.concatenate(
                both, 0
            ).astype(BF)


def window_flags(valid_rows, rows, first_col):
    t = lax.broadcasted_iota(jnp.int32, (TOK, 128), 0)
    lane = lax.broadcasted_iota(jnp.int32, (TOK, 128), 1)
    count = len(rows)
    tall = jnp.zeros((TOK, 128), F32)
    at = lane - first_col
    for half in range(TOK // (count * WIN_W)):
        for r, row in enumerate(rows):
            low = (half * count + r) * WIN_W
            here = (t >= low) & (t < low + WIN_W) & (at == t - low + half * WIN_W)
            tall = jnp.where(here, row, tall)
    return jnp.broadcast_to(jnp.sum(tall, axis=1, keepdims=True), (TOK, 128))


def kernel(
    tok_hbm, valid_ref, wqkv_hbm, wout_hbm, wup_hbm, wdown_hbm, p0, p1, p1t, pp, ppt, sets,
    out_ref,
    tok, ext, yext, ret, vhalo, wqkv, wout, wup, wdown, qkv, mixed, wide, hidden, flags,
    tok_sem, w_sem, halo_s, halo_r, row_s, row_r, diag_s, diag_r, v_s, v_r,
    ret_s, ret_r, corner_s, corner_r, below_s, below_r,
):
    lat, lon = lax.axis_index("lat"), lax.axis_index("lon")
    lats, lons = lax.axis_size("lat"), lax.axis_size("lon")
    north, south = lat == 0, lat == lats - 1
    left, right = lax.rem(lon + lons - 1, lons), lax.rem(lon + 1, lons)

    def tok_copy(p):
        return pltpu.make_async_copy(tok_hbm.at[pl.ds(12 * p, 12)], tok.at[pl.ds(12 * p, 12)], tok_sem.at[p])

    weights = [
        [
            pltpu.make_async_copy(src.at[b], dst.at[b], w_sem.at[b, n])
            for n, (src, dst) in enumerate(
                ((wqkv_hbm, wqkv), (wout_hbm, wout), (wup_hbm, wup), (wdown_hbm, wdown))
            )
        ]
        for b in range(2)
    ]
    tok_copy(3).start()
    weights[0][0].start()
    weights[0][1].start()
    weights[0][2].start()
    weights[0][3].start()
    for p in range(3):
        tok_copy(p).start()
    for n in range(4):
        weights[1][n].start()

    up, down = lax.rem(lat + lats - 1, lats), lax.rem(lat + 1, lats)
    barrier = pltpu.get_barrier_semaphore()
    for partner in ((lat, left), (lat, right), (up, lon), (up, right), (down, lon), (down, left)):
        pl.semaphore_signal(barrier, inc=1, device_id={"lat": partner[0], "lon": partner[1]}, device_id_type=MESH)

    qkv[:, TOK:PAD, :] = jnp.zeros((8, PAD - TOK, 1536), BF)

    @pl.when(north)
    def _():
        ext[0:3] = jnp.zeros((3, EXT, 512), BF)

    def send(src, dst, ssem, rsem, target):
        place = {"lat": target[0], "lon": target[1]}
        return pltpu.make_async_remote_copy(
            src_ref=src, dst_ref=dst, send_sem=ssem, recv_sem=rsem, device_id=place, device_id_type=MESH
        )

    v_copy = send(valid_ref.at[pl.ds(40, 8)], vhalo, v_s, v_r, (lat, left))

    def halo_copy(p):
        rows = pl.ds(3 + 12 * p, 12)
        return send(
            ext.at[rows, pl.ds(0, HALO)], ext.at[rows, pl.ds(48, HALO)], halo_s.at[p], halo_r.at[p], (lat, left)
        )

    row_copy = send(
        ext.at[pl.ds(48, 3), pl.ds(0, 48)], ext.at[pl.ds(0, 3), pl.ds(0, 48)], row_s, row_r, (lat + 1, lon)
    )
    diag_copy = send(
        ext.at[pl.ds(48, 3), pl.ds(0, HALO)], ext.at[pl.ds(0, 3), pl.ds(48, HALO)], diag_s, diag_r, (lat + 1, left)
    )

    def ret_copy(p, low, size):
        rows = pl.ds(low, size)
        return send(yext.at[rows, pl.ds(48, HALO)], ret.at[rows], ret_s.at[p], ret_r.at[p], (lat, right))

    below_copy = send(
        yext.at[pl.ds(0, 3), pl.ds(0, 48)], yext.at[pl.ds(48, 3), pl.ds(0, 48)], below_s, below_r, (lat - 1, lon)
    )
    corner_copy = send(
        yext.at[pl.ds(0, 3), pl.ds(48, HALO)], ret.at[pl.ds(48, 3)], corner_s, corner_r, (lat - 1, right)
    )
    pole_copy = send(
        yext.at[pl.ds(48, 3), pl.ds(48, HALO)], ret.at[pl.ds(48, 3)], corner_s, corner_r, (lat, right)
    )

    def project(b, x, tokens):
        width = tokens // TOK
        wide[0:tokens] = x
        out = jnp.dot(layer_norm(x), wqkv[b], preferred_element_type=F32)
        for w in range(width):
            qkv[w, 0:TOK, :] = out[TOK * w : TOK * w + TOK].astype(BF)

    def feed(b, tokens):
        resid = wide[0:tokens] + jnp.dot(mixed[0:tokens], wout[b], preferred_element_type=F32)
        resid = resid.astype(BF)
        normed = layer_norm(resid.astype(F32))
        for n in range(4):
            cut = slice(512 * n, 512 * n + 512)
            hidden[0:tokens, cut] = gelu(jnp.dot(normed, wup[b, :, cut], preferred_element_type=F32)).astype(BF)
        down = jnp.dot(hidden[0:tokens], wdown[b], preferred_element_type=F32)
        return (resid.astype(F32) + down).astype(BF)

    weights[0][0].wait()

    def block0(step, carry):
        p = lax.rem(step + 3, 4)
        tok_copy(p).wait()
        for band in range(2):
            x = tok[pl.ds(12 * p + 6 * band, 6)].reshape(288, 512)
            wide[288 * band : 288 * band + 288] = jnp.dot(p0[...], x, preferred_element_type=F32)
        project(0, wide[...], 576)
        masked = south & (p == 3)

        @pl.when(~masked)
        def _():
            attention(qkv, mixed, sets, 8)

        @pl.when(masked)
        def _():
            rows = [valid_wide(r) for r in range(2, 8)]
            for w in range(4):
                flags[w] = jnp.ones((TOK, 128), F32)
                flags[4 + w] = window_flags(None, rows, 12 * w)
            attention(qkv, mixed, sets, 8, flags)

        @pl.when(step == 0)
        def _():
            for n in range(1, 4):
                weights[0][n].wait()

        y = feed(0, 576)
        for band in range(2):
            nat = lax.dot_general(
                p0[...], y[288 * band : 288 * band + 288], (((0,), (0,)), ((), ())), preferred_element_type=F32
            )
            ext[pl.ds(3 + 12 * p + 6 * band, 6), 0:48] = nat.astype(BF).reshape(6, 48, 512)

        @pl.when(step == 0)
        def _():
            v_copy.start()

            @pl.when(~south)
            def _():
                row_copy.start()
                diag_copy.start()

        halo_copy(p).start()
        return carry

    def valid_wide(r):
        return vflag[r : r + 1, :]

    vflag = vhalo_flags(valid_ref, None)
    pl.semaphore_wait(barrier, 6)
    lax.fori_loop(0, 4, block0, 0)

    for n in range(4):
        weights[1][n].wait()
    v_copy.wait()
    vflag1 = vhalo_flags(valid_ref, vhalo)

    def block1(p, carry):
        @pl.when((p == 0) & ~north)
        def _():
            row_copy.wait_recv()
            diag_copy.wait_recv()

        halo_copy(p).wait_recv()
        for band in range(2):
            x = ext[pl.ds(12 * p + 6 * band, 6)].reshape(6 * EXT, 512)
            wide[288 * band : 288 * band + 288] = jnp.dot(p1[...], x, preferred_element_type=F32)
        project(1, wide[...], 576)
        masked = (south & (p == 3)) | (north & (p == 0))

        @pl.when(~masked)
        def _():
            attention(qkv, mixed, sets, 8)

        @pl.when(masked)
        def _():
            one = jnp.ones((1, 128), F32)
            top = one * jnp.where(north & (p == 0), 0.0, 1.0)
            tail = [jnp.where(p == 3, vflag1[r : r + 1, :], 1.0) for r in range(5)]
            for w in range(4):
                flags[w] = window_flags(None, [top] * 3 + [one] * 3, 6 + 12 * w)
                flags[4 + w] = window_flags(None, [one] + tail, 6 + 12 * w)
            attention(qkv, mixed, sets, 8, flags)

        y = feed(1, 576)
        for band in range(2):
            nat = jnp.dot(p1t[...], y[288 * band : 288 * band + 288], preferred_element_type=F32)
            yext[pl.ds(12 * p + 6 * band, 6)] = nat.astype(BF).reshape(6, EXT, 512)

        @pl.when(p == 0)
        def _():
            ret_copy(0, 3, 9).start()

            @pl.when(~north)
            def _():
                below_copy.start()
                corner_copy.start()

        @pl.when(p > 0)
        def _():
            ret_copy(p, 12 * p, 12).start()

        return carry

    lax.fori_loop(0, 4, block1, 0)

    @pl.when(south)
    def _():
        x = ext[48:51].reshape(3 * EXT, 512)
        wide[0:144] = jnp.dot(pp[...], x, preferred_element_type=F32)
        project(1, wide[0:144], 144)
        for w in range(2):
            flags[w] = window_flags(None, [vflag1[r : r + 1, :] for r in range(5, 8)], 6 + 24 * w)
        attention(qkv, mixed, sets, 2, flags, halves=True)
        y = feed(1, 144)
        nat = jnp.dot(ppt[...], y, preferred_element_type=F32)
        yext[48:51] = nat.astype(BF).reshape(3, EXT, 512)
        pole_copy.start()
        pole_copy.wait()

    @pl.when(~south)
    def _():
        below_copy.wait_recv()
        corner_copy.wait_recv()

    ret_copy(0, 3, 9).wait_recv()
    for p in range(1, 4):
        ret_copy(p, 12 * p, 12).wait_recv()
    col = lax.broadcasted_iota(jnp.int32, (1, HALO, 512), 1)

    def merge(p, carry):
        rows = pl.ds(3 + 8 * p, 8)
        here = pl.ds(8 * p, 8)
        out_ref[here, HALO:48] = yext[rows, HALO:48]
        out_ref[here, 0:HALO] = jnp.where(
            col < 6, ret[rows].astype(F32), yext[rows, 0:HALO].astype(F32)
        ).astype(BF)
        return carry

    lax.fori_loop(0, 6, merge, 0)
    lane = lax.broadcasted_iota(jnp.int32, (48, 128), 1)
    sub = lax.broadcasted_iota(jnp.int32, (48, 128), 0)
    for r in range(8):
        keep = jnp.sum(jnp.where(lane == sub, vflag1[r : r + 1, :], 0.0), axis=1, keepdims=True)
        out_ref[40 + r] = (out_ref[40 + r].astype(F32) * keep).astype(BF)

    for p in range(4):
        halo_copy(p).wait_send()
    ret_copy(0, 3, 9).wait_send()
    for p in range(1, 4):
        ret_copy(p, 12 * p, 12).wait_send()

    @pl.when(~south)
    def _():
        row_copy.wait_send()
        diag_copy.wait_send()

    @pl.when(~north)
    def _():
        below_copy.wait_send()
        corner_copy.wait_send()


def vhalo_flags(valid_ref, vhalo):
    own = valid_ref[40:48, :].astype(F32)
    parts = [own]
    if vhalo is not None:
        parts.append(vhalo[:, 0:HALO].astype(F32))
        parts.append(jnp.zeros((8, 64), F32))
    else:
        parts.append(jnp.zeros((8, 80), F32))
    return jnp.concatenate(parts, axis=1)


def shards(tokens, valid, w_qkv, w_out, w_up, w_down):
    vmem = pl.BlockSpec(memory_space=pltpu.VMEM)
    hbm = pl.BlockSpec(memory_space=pl.ANY)
    dma = pltpu.SemaphoreType.DMA
    take0 = to_window_order(6, 48, 0, 6)
    take1 = to_window_order(6, EXT, 6, 6)
    take_pole = to_window_order(3, EXT, 6, 3)
    constants = [jnp.asarray(a, BF) for a in (take0, take1, take1.T, take_pole, take_pole.T, head_sets())]
    return pl.pallas_call(
        kernel,
        out_shape=jax.ShapeDtypeStruct((48, 48, 512), BF),
        in_specs=[hbm, vmem] + [hbm] * 4 + [vmem] * 6,
        out_specs=vmem,
        scratch_shapes=[
            pltpu.VMEM((48, 48, 512), BF),
            pltpu.VMEM((51, EXT, 512), BF),
            pltpu.VMEM((51, EXT, 512), BF),
            pltpu.VMEM((51, HALO, 512), BF),
            pltpu.VMEM((8, 48), jnp.int32),
            pltpu.VMEM((2, 512, 1536), BF),
            pltpu.VMEM((2, 512, 512), BF),
            pltpu.VMEM((2, 512, 2048), BF),
            pltpu.VMEM((2, 2048, 512), BF),
            pltpu.VMEM((8, PAD, 1536), BF),
            pltpu.VMEM((576, 512), BF),
            pltpu.VMEM((576, 512), F32),
            pltpu.VMEM((576, 2048), BF),
            pltpu.VMEM((8, TOK, 128), F32),
            dma((4,)), dma((2, 4)), dma((4,)), dma((4,)), dma(()), dma(()), dma(()), dma(()), dma(()), dma(()),
            dma((4,)), dma((4,)), dma(()), dma(()), dma(()), dma(()),
        ],
        compiler_params=pltpu.CompilerParams(
            collective_id=0, has_side_effects=True, vmem_limit_bytes=60 << 20
        ),
        name="swin",
    )(tokens, valid, w_qkv, w_out, w_up, w_down, *constants)


def solution(mesh):
    return jax.shard_map(
        shards,
        mesh=mesh,
        in_specs=(P("lat", "lon", None), P("lat", "lon"), P(), P(), P(), P()),
        out_specs=P("lat", "lon", None),
        check_vma=False,
    )
```

time: 580 us -> 85.7 us (0.15)
  the two profiles are of different devices: /device:TPU:24 before, /device:TPU:28 now
where the time goes in v1:
time: 85.7 us; the launch traced here: 84.4 us
  Pallas kernels  81.1 us (95%)
  local copies, waits for them, and re-layouts  3.23 us (4%)
    pallas_call x1, Pallas kernels, shards(): pl.pallas_call(kernel, out_shape=jax.ShapeDtypeStruct((48, 48, 512), BF),...  81.1 us
    unnamed x1, local copies, waits for them, and re-layouts  3.23 us

profile of v1, /device:TPU:28, one launch (start us, length us, event | category | flops | bytes accessed | tf_op | source)
XLA Modules:
  0.0 84.4 jit_solution(7467121601012153557)
XLA Ops:
  0.0 81.1 %swin.1 = bf16[48,48,512]{2,1,0:T(8,128)(2,1)} custom-call(bf16[48,48,512]{2,1,0:T(8,128)(2,1)} %tok_hbm.1, s32[48,48]{1,0:T(8,128)} %valid_ref.1, bf16[2,512,1536]{2,1,0:T(8,128)(2,1)} %wqkv_hbm.1, bf16[2,512,512]{2,1,0:T(8,128)(2,1)} %wout_hbm.1, bf16[2,512,2048]{2,1,0:T(8,128)(2,1)} %wup_hbm.1, bf16[2,2048,512]{2,1,0:T(8,128)(2,1)} %wdown_hbm.1, ...), custom_call_target="tpu_custom_call" | custom-call | tf_op jit(solution)/shard_map/swin/pallas_call | solution.py:390
  81.1 3.2 %copy.14 = bf16[48,48,512]{2,1,0:T(8,128)(2,1)} copy(bf16[48,48,512]{2,1,0:T(8,128)(2,1)} %swin.1) | data formatting | bytes 4718592

commit v2 on v1

v2 whole, which is shorter than its diff:
```python
import jax
import jax.numpy as jnp
import numpy as np
from jax import lax
from jax.experimental import pallas as pl
from jax.experimental.pallas import tpu as pltpu
from jax.sharding import PartitionSpec as P

HEADS = 16
WIN_H = 6
WIN_W = 12
TOK = WIN_H * WIN_W
PAD = 80
EXT = 64
HALO = 16
MESH = pl.DeviceIdType.MESH
BF = jnp.bfloat16
F32 = jnp.float32


ORDER = [(0, 3), (1, 3), (0, 0), (0, 1), (0, 2), (1, 0), (1, 1), (1, 2)]


def head_sets():
    head = np.arange(256) // 32
    return np.stack([head // 3 == i for i in range(3)] + [head % 3 == j for j in range(3)])[:, None, :]


def layer_norm(wide):
    center = wide - jnp.mean(wide, axis=-1, keepdims=True)
    spread = jnp.mean(center * center, axis=-1, keepdims=True)
    return (center * lax.rsqrt(spread + 1e-05)).astype(BF)


def gelu(x):
    half = 0.5 * x
    return half + half * jnp.tanh(x * (0.7978845608028654 + 0.035677408136300125 * (x * x)))


def half_heads(q, k, v, sets, bias):
    by_key = jnp.concatenate([k * sets[i] for i in range(3)], 0)
    by_query = jnp.concatenate([q * sets[3 + j] for j in range(3)], 0)
    scores = lax.dot_general(by_key, by_query, (((1,), (1,)), ((), ())), preferred_element_type=F32)
    parts = []
    for i in range(3):
        part = scores[PAD * i : PAD * i + TOK] + bias
        largest = jnp.max(part, axis=0, keepdims=True)
        expo = jnp.exp2((part - largest) * (1.4426950408889634 * 32**-0.5))
        total = jnp.sum(expo, axis=0, keepdims=True)
        parts += [expo * (1.0 / total), jnp.zeros((PAD - TOK, 3 * PAD), F32)]
    probs = jnp.concatenate(parts, 0).astype(BF)
    by_value = jnp.concatenate([v * sets[i] for i in range(3)], 0)
    mixed = lax.dot_general(probs, by_value, (((0,), (0,)), ((), ())), preferred_element_type=F32)
    pick = [sets[3 + j].astype(F32) for j in range(3)]
    return (
        mixed[:TOK] * pick[0] + mixed[PAD : PAD + TOK] * pick[1] + mixed[2 * PAD : 2 * PAD + TOK] * pick[2]
    )


def window_bias(rows, first_col, halves=False):
    t = lax.broadcasted_iota(jnp.int32, (TOK, 128), 0)
    lane = lax.broadcasted_iota(jnp.int32, (TOK, 128), 1)
    tall = jnp.zeros((TOK, 128), F32)
    at = lane - first_col
    for half in range(2 if halves else 1):
        for r, row in enumerate(rows):
            low = (half * len(rows) + r) * WIN_W
            here = (t >= low) & (t < low + WIN_W) & (at == t - low + half * WIN_W)
            tall = jnp.where(here, row, tall)
    flag = jnp.sum(tall, axis=1, keepdims=True)
    key = lax.broadcasted_iota(jnp.int32, (TOK, 256), 0)
    query = lax.broadcasted_iota(jnp.int32, (TOK, 256), 1)
    query = query - PAD * ((query >= PAD).astype(jnp.int32) + (query >= 2 * PAD).astype(jnp.int32))
    allow = flag > 0.5
    if halves:
        allow = allow & ((key < TOK // 2) == (query < TOK // 2))
    allow = allow | (key == query) | (query >= TOK)
    return jnp.where(allow, 0.0, -jnp.inf)


def kernel(
    tok_hbm, valid_ref, wqkv_hbm, wout_hbm, wup_hbm, wdown_hbm, sets_ref,
    out_hbm,
    tok, ext, yext, ret, vhalo, wqkv, wout, wup, wdown, qkv, mixed, wide, resid, hidden, bias,
    tok_sem, w_sem, out_sem, halo_s, halo_r, row_s, row_r, diag_s, diag_r, v_s, v_r,
    ret_s, ret_r, corner_s, corner_r, below_s, below_r,
):
    lat, lon = lax.axis_index("lat"), lax.axis_index("lon")
    lats, lons = lax.axis_size("lat"), lax.axis_size("lon")
    north, south = lat == 0, lat == lats - 1
    left, right = lax.rem(lon + lons - 1, lons), lax.rem(lon + 1, lons)

    def tok_copy(p):
        return pltpu.make_async_copy(tok_hbm.at[pl.ds(12 * p, 12)], tok.at[pl.ds(12 * p, 12)], tok_sem.at[p])

    weights = [
        [
            pltpu.make_async_copy(src.at[b], dst.at[b], w_sem.at[b, n])
            for n, (src, dst) in enumerate(
                ((wqkv_hbm, wqkv), (wout_hbm, wout), (wup_hbm, wup), (wdown_hbm, wdown))
            )
        ]
        for b in range(2)
    ]
    tok_copy(3).start()
    for n in range(4):
        weights[0][n].start()
    for p in range(3):
        tok_copy(p).start()
    for n in range(4):
        weights[1][n].start()

    up, down = lax.rem(lat + lats - 1, lats), lax.rem(lat + 1, lats)
    barrier = pltpu.get_barrier_semaphore()
    for partner in ((lat, left), (lat, right), (up, lon), (up, right), (down, lon), (down, left)):
        place = {"lat": partner[0], "lon": partner[1]}
        pl.semaphore_signal(barrier, inc=1, device_id=place, device_id_type=MESH)

    qkv[:, TOK:PAD, :] = jnp.zeros((8, PAD - TOK, 1536), BF)
    bias[...] = jnp.zeros((8, TOK, 256), F32)

    @pl.when(north)
    def _():
        ext[0:3] = jnp.zeros((3, EXT, 512), BF)

    def send(src, dst, ssem, rsem, target):
        place = {"lat": target[0], "lon": target[1]}
        return pltpu.make_async_remote_copy(
            src_ref=src, dst_ref=dst, send_sem=ssem, recv_sem=rsem, device_id=place, device_id_type=MESH
        )

    v_copy = send(valid_ref.at[pl.ds(40, 8)], vhalo, v_s, v_r, (lat, left))

    def halo_copy(p):
        rows = pl.ds(3 + 12 * p, 12)
        return send(
            ext.at[rows, pl.ds(0, HALO)], ext.at[rows, pl.ds(48, HALO)], halo_s.at[p], halo_r.at[p], (lat, left)
        )

    row_copy = send(
        ext.at[pl.ds(48, 3), pl.ds(0, 48)], ext.at[pl.ds(0, 3), pl.ds(0, 48)], row_s, row_r, (lat + 1, lon)
    )
    diag_copy = send(
        ext.at[pl.ds(48, 3), pl.ds(0, HALO)], ext.at[pl.ds(0, 3), pl.ds(48, HALO)], diag_s, diag_r, (lat + 1, left)
    )

    def ret_copy(p, low, size):
        rows = pl.ds(low, size)
        return send(yext.at[rows, pl.ds(48, HALO)], ret.at[rows], ret_s.at[p], ret_r.at[p], (lat, right))

    below_copy = send(
        yext.at[pl.ds(0, 3), pl.ds(0, 48)], yext.at[pl.ds(48, 3), pl.ds(0, 48)], below_s, below_r, (lat - 1, lon)
    )
    corner_copy = send(
        yext.at[pl.ds(0, 3), pl.ds(48, HALO)], ret.at[pl.ds(48, 3)], corner_s, corner_r, (lat - 1, right)
    )
    pole_copy = send(
        yext.at[pl.ds(48, 3), pl.ds(48, HALO)], ret.at[pl.ds(48, 3)], corner_s, corner_r, (lat, right)
    )

    def out_copy(n, low, size):
        return pltpu.make_async_copy(
            yext.at[pl.ds(low, size), pl.ds(0, 48)], out_hbm.at[pl.ds(low - 3, size)], out_sem.at[n]
        )

    sets = [sets_ref[i] for i in range(6)]

    def gather0(p):
        x = tok[pl.ds(12 * p, 12)].astype(F32)
        for w, (band, j) in enumerate(ORDER):
            wide[TOK * w : TOK * w + TOK] = jnp.concatenate(
                [x[6 * band + r, 12 * j : 12 * j + 12] for r in range(6)], 0
            )

    def gather1(p):
        x = ext[pl.ds(12 * p, 12)].astype(F32)
        for w, (band, j) in enumerate(ORDER):
            wide[TOK * w : TOK * w + TOK] = jnp.concatenate(
                [x[6 * band + r, 12 * j + 6 : 12 * j + 18] for r in range(6)], 0
            )

    def project(b, tokens):
        out = jnp.dot(layer_norm(wide[0:tokens]), wqkv[b], preferred_element_type=F32)
        for w in range(tokens // TOK):
            qkv[w, 0:TOK, :] = out[TOK * w : TOK * w + TOK].astype(BF)

    def attend(pair):
        for g in range(2):
            both = []
            for w in (2 * pair, 2 * pair + 1):
                q = qkv[w, :, 256 * g : 256 * g + 256]
                k = qkv[w, :, 512 + 256 * g : 768 + 256 * g]
                v = qkv[w, :, 1024 + 256 * g : 1280 + 256 * g]
                both.append(half_heads(q, k, v, sets, bias[w, :, 0 : 3 * PAD]))
            mixed[2 * TOK * pair : 2 * TOK * pair + 2 * TOK, 256 * g : 256 * g + 256] = jnp.concatenate(
                both, 0
            ).astype(BF)

    def add_mixed(b, rows):
        total = wide[rows] + jnp.dot(mixed[rows], wout[b], preferred_element_type=F32)
        total = total.astype(BF)
        resid[rows] = total
        return layer_norm(total.astype(F32))

    def expand(b, normed, rows, n):
        cut = slice(512 * n, 512 * n + 512)
        hidden[rows, cut] = gelu(jnp.dot(normed, wup[b, :, cut], preferred_element_type=F32)).astype(BF)

    def contract(b, rows):
        return resid[rows].astype(F32) + jnp.dot(hidden[rows], wdown[b], preferred_element_type=F32)

    def scatter0(y, p):
        rows = [
            y[TOK * w + 12 * r : TOK * w + 12 * r + 12]
            for band in range(2)
            for r in range(6)
            for w in (ORDER.index((band, j)) for j in range(4))
        ]
        ext[pl.ds(3 + 12 * p, 12), 0:48] = jnp.concatenate(rows, 0).astype(BF).reshape(12, 48, 512)

    def scatter1(y, p):
        for band in range(2):
            for r in range(6):
                row = [y[TOK * w + 12 * r : TOK * w + 12 * r + 12] for w in (ORDER.index((band, j)) for j in range(4))]
                row = [jnp.zeros((6, 512), F32)] + row + [jnp.zeros((10, 512), F32)]
                yext[12 * p + 6 * band + r] = jnp.concatenate(row, 0).astype(BF)

    everything = slice(0, 576)

    def step(b_feed, p_feed, b_att, gather, p_att, scatter):
        normed = add_mixed(b_feed, everything)
        gather(p_att)
        project(b_att, 576)
        for n in range(4):
            expand(b_feed, normed, everything, n)
            attend(n)
        scatter(contract(b_feed, everything), p_feed)

    vflag = flag_rows(valid_ref, None)

    @pl.when(south)
    def _():
        for w, (band, j) in enumerate(ORDER):
            if band == 1:
                bias[w] = window_bias([vflag[r : r + 1] for r in range(2, 8)], 12 * j)

    tok_copy(3).wait()
    weights[0][0].wait()
    gather0(3)
    project(0, 576)
    for n in range(4):
        attend(n)

    @pl.when(south)
    def _():
        for w, (band, j) in enumerate(ORDER):
            if band == 1:
                bias[w] = jnp.zeros((TOK, 256), F32)

    for n in range(1, 4):
        weights[0][n].wait()
    pl.semaphore_wait(barrier, 6)
    v_copy.start()

    def block0(p, carry):
        tok_copy(p).wait()
        before = lax.rem(p + 3, 4)
        step(0, before, 0, gather0, p, scatter0)

        @pl.when((p == 0) & ~south)
        def _():
            row_copy.start()
            diag_copy.start()

        halo_copy(before).start()
        return carry

    lax.fori_loop(0, 3, block0, 0)

    v_copy.wait()
    vflag = flag_rows(valid_ref, vhalo)
    one = jnp.ones((1, 128), F32)
    for n in range(4):
        weights[1][n].wait()

    @pl.when(north)
    def _():
        for w, (band, j) in enumerate(ORDER):
            if band == 0:
                bias[w] = window_bias([0.0 * one] * 3 + [one] * 3, 6 + 12 * j)

    @pl.when(~north)
    def _():
        row_copy.wait_recv()
        diag_copy.wait_recv()

    halo_copy(3).wait_recv()
    halo_copy(0).wait_recv()
    step(0, 2, 1, gather1, 0, scatter0)
    halo_copy(2).start()

    @pl.when(north)
    def _():
        for w, (band, j) in enumerate(ORDER):
            if band == 0:
                bias[w] = jnp.zeros((TOK, 256), F32)

    def merge(low, size):
        rows = pl.ds(low, size)
        col = lax.broadcasted_iota(jnp.int32, (1, HALO, 512), 1)
        yext[rows, 0:HALO] = jnp.where(
            col < 6, ret[rows].astype(F32), yext[rows, 0:HALO].astype(F32)
        ).astype(BF)

    def block1(p, carry):
        @pl.when(p < 3)
        def _():
            halo_copy(p).wait_recv()

        @pl.when(south & (p == 3))
        def _():
            for w, (band, j) in enumerate(ORDER):
                if band == 1:
                    bias[w] = window_bias([one] + [vflag[r : r + 1] for r in range(5)], 6 + 12 * j)

        step(1, p - 1, 1, gather1, p, scatter1)

        @pl.when(p == 1)
        def _():
            ret_copy(0, 3, 9).start()

            @pl.when(~north)
            def _():
                below_copy.start()
                corner_copy.start()

        @pl.when(p == 2)
        def _():
            ret_copy(1, 12, 12).start()
            ret_copy(0, 3, 9).wait_recv()
            merge(3, 9)
            out_copy(0, 3, 9).start()

        @pl.when(p == 3)
        def _():
            ret_copy(2, 24, 12).start()
            ret_copy(1, 12, 12).wait_recv()
            merge(12, 12)
            out_copy(1, 12, 12).start()

        return carry

    lax.fori_loop(1, 4, block1, 0)

    first, others = slice(0, 2 * TOK), slice(2 * TOK, 8 * TOK)
    normed = add_mixed(1, first)
    for n in range(4):
        expand(1, normed, first, n)
    y = contract(1, first)
    for band in range(2):
        for r in range(6):
            row = [y[TOK * band + 12 * r + 6 : TOK * band + 12 * r + 12], jnp.zeros((10, 512), F32)]
            yext[36 + 6 * band + r, 48:64] = jnp.concatenate(row, 0).astype(BF)
    ret_copy(3, 36, 12).start()
    normed = add_mixed(1, others)
    for n in range(4):
        expand(1, normed, others, n)
    y = jnp.concatenate([y, contract(1, others)], 0)
    for band in range(2):
        for r in range(6):
            row = [y[TOK * w + 12 * r : TOK * w + 12 * r + 12] for w in (ORDER.index((band, j)) for j in range(4))]
            row = [jnp.zeros((6, 512), F32)] + row
            yext[36 + 6 * band + r, 0:48] = jnp.concatenate(row, 0)[0:48].astype(BF)

    @pl.when(south)
    def _():
        x = ext[48:51].astype(F32)
        for w in range(2):
            wide[TOK * w : TOK * w + TOK] = jnp.concatenate(
                [x[r, 12 * j + 6 : 12 * j + 18] for j in (2 * w, 2 * w + 1) for r in range(3)], 0
            )
            bias[w] = window_bias([vflag[r : r + 1] for r in range(5, 8)], 6 + 24 * w, halves=True)
        project(1, 2 * TOK)
        attend(0)
        normed = add_mixed(1, first)
        for n in range(4):
            expand(1, normed, first, n)
        y = contract(1, first)
        for r in range(3):
            row = [y[36 * j + 12 * r : 36 * j + 12 * r + 12] for j in range(4)]
            row = [jnp.zeros((6, 512), F32)] + row + [jnp.zeros((10, 512), F32)]
            yext[48 + r] = jnp.concatenate(row, 0).astype(BF)
        pole_copy.start()
        pole_copy.wait()

    @pl.when(~south)
    def _():
        below_copy.wait_recv()
        corner_copy.wait_recv()

    ret_copy(2, 24, 12).wait_recv()
    merge(24, 12)
    out_copy(2, 24, 12).start()
    ret_copy(3, 36, 12).wait_recv()
    merge(36, 15)
    lane = lax.broadcasted_iota(jnp.int32, (48, 128), 1)
    sub = lax.broadcasted_iota(jnp.int32, (48, 128), 0)
    for r in range(8):
        keep = jnp.sum(jnp.where(lane == sub, vflag[r : r + 1], 0.0), axis=1, keepdims=True)
        yext[43 + r, 0:48] = (yext[43 + r, 0:48].astype(F32) * keep).astype(BF)
    out_copy(3, 36, 15).start()

    for p in range(4):
        halo_copy(p).wait_send()
    ret_copy(0, 3, 9).wait_send()
    for p in range(1, 4):
        ret_copy(p, 12 * p, 12).wait_send()

    @pl.when(~south)
    def _():
        row_copy.wait_send()
        diag_copy.wait_send()

    @pl.when(~north)
    def _():
        below_copy.wait_send()
        corner_copy.wait_send()

    out_copy(0, 3, 9).wait()
    out_copy(1, 12, 12).wait()
    out_copy(2, 24, 12).wait()
    out_copy(3, 36, 15).wait()


def flag_rows(valid_ref, vhalo):
    parts = [valid_ref[40:48, :].astype(F32)]
    if vhalo is not None:
        parts += [vhalo[:, 0:HALO].astype(F32), jnp.zeros((8, 64), F32)]
    else:
        parts.append(jnp.zeros((8, 80), F32))
    return jnp.concatenate(parts, axis=1)


def deliver(src, dst, sem):
    copies = [
        pltpu.make_async_copy(src.at[pl.ds(6 * n, 6)], dst.at[pl.ds(6 * n, 6)], sem.at[n]) for n in range(8)
    ]
    for copy in copies:
        copy.start()
    for copy in copies:
        copy.wait()


def shards(tokens, valid, w_qkv, w_out, w_up, w_down):
    vmem = pl.BlockSpec(memory_space=pltpu.VMEM)
    hbm = pl.BlockSpec(memory_space=pl.ANY)
    dma = pltpu.SemaphoreType.DMA
    result = jax.ShapeDtypeStruct((48, 48, 512), BF)
    done = pl.pallas_call(
        kernel,
        out_shape=result,
        in_specs=[hbm, vmem] + [hbm] * 4 + [vmem],
        out_specs=hbm,
        scratch_shapes=[
            pltpu.VMEM((48, 48, 512), BF),
            pltpu.VMEM((51, EXT, 512), BF),
            pltpu.VMEM((51, EXT, 512), BF),
            pltpu.VMEM((51, HALO, 512), BF),
            pltpu.VMEM((8, 48), jnp.int32),
            pltpu.VMEM((2, 512, 1536), BF),
            pltpu.VMEM((2, 512, 512), BF),
            pltpu.VMEM((2, 512, 2048), BF),
            pltpu.VMEM((2, 2048, 512), BF),
            pltpu.VMEM((8, PAD, 1536), BF),
            pltpu.VMEM((576, 512), BF),
            pltpu.VMEM((576, 512), F32),
            pltpu.VMEM((576, 512), BF),
            pltpu.VMEM((576, 2048), BF),
            pltpu.VMEM((8, TOK, 256), F32),
            dma((4,)), dma((2, 4)), dma((4,)),
            dma((4,)), dma((4,)), dma(()), dma(()), dma(()), dma(()), dma(()), dma(()),
            dma((4,)), dma((4,)), dma(()), dma(()), dma(()), dma(()),
        ],
        compiler_params=pltpu.CompilerParams(
            collective_id=0, has_side_effects=True, vmem_limit_bytes=60 << 20
        ),
        name="swin",
    )(tokens, valid, w_qkv, w_out, w_up, w_down, jnp.asarray(head_sets(), BF))
    return pl.pallas_call(
        deliver,
        out_shape=result,
        in_specs=[hbm],
        out_specs=hbm,
        scratch_shapes=[dma((8,))],
        name="deliver",
    )(done)


def solution(mesh):
    return jax.shard_map(
        shards,
        mesh=mesh,
        in_specs=(P("lat", "lon", None), P("lat", "lon"), P(), P(), P(), P()),
        out_specs=P("lat", "lon", None),
        check_vma=False,
    )
```

time: 85.7 us -> 140 us (1.63)
  Pallas kernels: 81.1 us -> 140 us
  local copies, waits for them, and re-layouts: 3.23 us -> 0 us
    pallas_call x1 -> x2, Pallas kernels: 81.1 us -> 140 us  [the longest x1 72.6 us: shards(): pl.pallas_call(deliver, out_shape=result, in_specs=[hbm], out_specs=hbm,...]
    unnamed x1 -> x0, local copies, waits for them, and re-layouts: 3.23 us -> none
where the time goes in v2:
time: 140 us
  Pallas kernels  140 us (100%)
    pallas_call x1, Pallas kernels, shards(): pl.pallas_call(deliver, out_shape=result, in_specs=[hbm], out_specs=hbm,...  72.6 us
    pallas_call x1, Pallas kernels, shards(): pl.pallas_call(kernel, out_shape=result, in_specs=[hbm, vmem] + [hbm] * 4...  67.1 us

profile of v2, /device:TPU:28, one launch (start us, length us, event | category | flops | bytes accessed | tf_op | source)
XLA Modules:
  0.0 140.0 jit_solution(5850905325936760466)
XLA Ops:
  0.0 67.1 %swin.1.src = bf16[48,48,512]{2,1,0:T(8,128)(2,1)} custom-call(bf16[48,48,512]{2,1,0:T(8,128)(2,1)} %tok_hbm.1, s32[48,48]{1,0:T(8,128)} %valid_ref.1, bf16[2,512,1536]{2,1,0:T(8,128)(2,1)} %wqkv_hbm.1, bf16[2,512,512]{2,1,0:T(8,128)(2,1)} %wout_hbm.1, bf16[2,512,2048]{2,1,0:T(8,128)(2,1)} %wup_hbm.1, bf16[2,2048,512]{2,1,0:T(8,128)(2,1)} %wdown_hbm.1, ...), custom_call_target="tpu_custom_call" | custom-call | tf_op jit(solution)/shard_map/swin/pallas_call | solution.py:459
  67.1 72.6 %deliver.1 = bf16[48,48,512]{2,1,0:T(8,128)(2,1)} custom-call(bf16[48,48,512]{2,1,0:T(8,128)(2,1)} %swin.1.src), custom_call_target="tpu_custom_call" | custom-call | tf_op jit(solution)/shard_map/deliver/pallas_call | solution.py:489

commit v3 on v2

--- a/solution.py
+++ b/solution.py
@@ -18,7 +18,8 @@
 F32 = jnp.float32
 
 
-ORDER = [(0, 3), (1, 3), (0, 0), (0, 1), (0, 2), (1, 0), (1, 1), (1, 2)]
+ORDER = [(0, 0), (0, 1), (0, 2), (1, 0), (1, 1), (1, 2), (0, 3), (1, 3)]
+SCALE = 1.4426950408889634 * 32**-0.5
 
 
 def head_sets():
@@ -32,9 +33,8 @@
     return (center * lax.rsqrt(spread + 1e-05)).astype(BF)
 
 
-def gelu(x):
-    half = 0.5 * x
-    return half + half * jnp.tanh(x * (0.7978845608028654 + 0.035677408136300125 * (x * x)))
+def twice_gelu(x):
+    return x + x * jnp.tanh(x * (0.7978845608028654 + 0.035677408136300125 * (x * x)))
 
 
 def half_heads(q, k, v, sets, bias):
@@ -43,9 +43,11 @@
     scores = lax.dot_general(by_key, by_query, (((1,), (1,)), ((), ())), preferred_element_type=F32)
     parts = []
     for i in range(3):
-        part = scores[PAD * i : PAD * i + TOK] + bias
+        part = scores[PAD * i : PAD * i + TOK]
+        if bias is not None:
+            part = part + bias
         largest = jnp.max(part, axis=0, keepdims=True)
-        expo = jnp.exp2((part - largest) * (1.4426950408889634 * 32**-0.5))
+        expo = jnp.exp2(part - largest)
         total = jnp.sum(expo, axis=0, keepdims=True)
         parts += [expo * (1.0 / total), jnp.zeros((PAD - TOK, 3 * PAD), F32)]
     probs = jnp.concatenate(parts, 0).astype(BF)
@@ -116,8 +118,8 @@
         place = {"lat": partner[0], "lon": partner[1]}
         pl.semaphore_signal(barrier, inc=1, device_id=place, device_id_type=MESH)
 
-    qkv[:, TOK:PAD, :] = jnp.zeros((8, PAD - TOK, 1536), BF)
-    bias[...] = jnp.zeros((8, TOK, 256), F32)
+    qkv[:, TOK:PAD, :] = jnp.zeros((10, PAD - TOK, 1536), BF)
+    bias[...] = jnp.zeros((10, TOK, 256), F32)
 
     @pl.when(north)
     def _():
@@ -179,19 +181,21 @@
                 [x[6 * band + r, 12 * j + 6 : 12 * j + 18] for r in range(6)], 0
             )
 
-    def project(b, tokens):
-        out = jnp.dot(layer_norm(wide[0:tokens]), wqkv[b], preferred_element_type=F32)
+    def project(b, x, tokens):
+        out = jnp.dot(layer_norm(x), wqkv[b], preferred_element_type=F32)
         for w in range(tokens // TOK):
-            qkv[w, 0:TOK, :] = out[TOK * w : TOK * w + TOK].astype(BF)
-
-    def attend(pair):
+            rows = slice(TOK * w, TOK * w + TOK)
+            qkv[w, 0:TOK, 0:512] = (out[rows, 0:512] * SCALE).astype(BF)
+            qkv[w, 0:TOK, 512:1536] = out[rows, 512:1536].astype(BF)
+
+    def attend(pair, masked):
         for g in range(2):
             both = []
             for w in (2 * pair, 2 * pair + 1):
                 q = qkv[w, :, 256 * g : 256 * g + 256]
                 k = qkv[w, :, 512 + 256 * g : 768 + 256 * g]
                 v = qkv[w, :, 1024 + 256 * g : 1280 + 256 * g]
-                both.append(half_heads(q, k, v, sets, bias[w, :, 0 : 3 * PAD]))
+                both.append(half_heads(q, k, v, sets, bias[w, :, 0 : 3 * PAD] if masked else None))
             mixed[2 * TOK * pair : 2 * TOK * pair + 2 * TOK, 256 * g : 256 * g + 256] = jnp.concatenate(
                 both, 0
             ).astype(BF)
@@ -204,10 +208,10 @@
 
     def expand(b, normed, rows, n):
         cut = slice(512 * n, 512 * n + 512)
-        hidden[rows, cut] = gelu(jnp.dot(normed, wup[b, :, cut], preferred_element_type=F32)).astype(BF)
+        hidden[rows, cut] = twice_gelu(jnp.dot(normed, wup[b, :, cut], preferred_element_type=F32)).astype(BF)
 
     def contract(b, rows):
-        return resid[rows].astype(F32) + jnp.dot(hidden[rows], wdown[b], preferred_element_type=F32)
+        return resid[rows].astype(F32) + 0.5 * jnp.dot(hidden[rows], wdown[b], preferred_element_type=F32)
 
     def scatter0(y, p):
         rows = [
@@ -227,13 +231,15 @@
 
     everything = slice(0, 576)
 
-    def step(b_feed, p_feed, b_att, gather, p_att, scatter):
+    def step(b_feed, p_feed, b_att, gather, p_att, scatter, masked=False, edge=False):
         normed = add_mixed(b_feed, everything)
         gather(p_att)
-        project(b_att, 576)
+        project(b_att, wide[0:720] if edge else wide[0:576], 720 if edge else 576)
         for n in range(4):
             expand(b_feed, normed, everything, n)
-            attend(n)
+            attend(n, masked)
+        if edge:
+            attend(4, masked)
         scatter(contract(b_feed, everything), p_feed)
 
     vflag = flag_rows(valid_ref, None)
@@ -247,9 +253,9 @@
     tok_copy(3).wait()
     weights[0][0].wait()
     gather0(3)
-    project(0, 576)
+    project(0, wide[0:576], 576)
     for n in range(4):
-        attend(n)
+        attend(n, True)
 
     @pl.when(south)
     def _():
@@ -296,7 +302,7 @@
 
     halo_copy(3).wait_recv()
     halo_copy(0).wait_recv()
-    step(0, 2, 1, gather1, 0, scatter0)
+    step(0, 2, 1, gather1, 0, scatter0, masked=True)
     halo_copy(2).start()
 
     @pl.when(north)
@@ -313,16 +319,7 @@
         ).astype(BF)
 
     def block1(p, carry):
-        @pl.when(p < 3)
-        def _():
-            halo_copy(p).wait_recv()
-
-        @pl.when(south & (p == 3))
-        def _():
-            for w, (band, j) in enumerate(ORDER):
-                if band == 1:
-                    bias[w] = window_bias([one] + [vflag[r : r + 1] for r in range(5)], 6 + 12 * j)
-
+        halo_copy(p).wait_recv()
         step(1, p - 1, 1, gather1, p, scatter1)
 
         @pl.when(p == 1)
@@ -341,18 +338,33 @@
             merge(3, 9)
             out_copy(0, 3, 9).start()
 
-        @pl.when(p == 3)
-        def _():
-            ret_copy(2, 24, 12).start()
-            ret_copy(1, 12, 12).wait_recv()
-            merge(12, 12)
-            out_copy(1, 12, 12).start()
-
         return carry
 
-    lax.fori_loop(1, 4, block1, 0)
-
-    first, others = slice(0, 2 * TOK), slice(2 * TOK, 8 * TOK)
+    lax.fori_loop(1, 3, block1, 0)
+
+    @pl.when(south)
+    def _():
+        for w, (band, j) in enumerate(ORDER):
+            if band == 1:
+                bias[w] = window_bias([one] + [vflag[r : r + 1] for r in range(5)], 6 + 12 * j)
+
+    for w in range(2):
+        bias[8 + w] = window_bias([vflag[r : r + 1] for r in range(5, 8)], 6 + 24 * w, halves=True)
+
+    def gather_last(p):
+        gather1(p)
+        x = ext[48:51].astype(F32)
+        wide[8 * TOK : 10 * TOK] = jnp.concatenate(
+            [x[r, 12 * j + 6 : 12 * j + 18] for j in range(4) for r in range(3)], 0
+        )
+
+    step(1, 2, 1, gather_last, 3, scatter1, masked=True, edge=True)
+    ret_copy(2, 24, 12).start()
+    ret_copy(1, 12, 12).wait_recv()
+    merge(12, 12)
+    out_copy(1, 12, 12).start()
+
+    others, first = slice(0, 6 * TOK), slice(6 * TOK, 10 * TOK)
     normed = add_mixed(1, first)
     for n in range(4):
         expand(1, normed, first, n)
@@ -361,11 +373,20 @@
         for r in range(6):
             row = [y[TOK * band + 12 * r + 6 : TOK * band + 12 * r + 12], jnp.zeros((10, 512), F32)]
             yext[36 + 6 * band + r, 48:64] = jnp.concatenate(row, 0).astype(BF)
+
+    @pl.when(south)
+    def _():
+        for r in range(3):
+            row = [y[2 * TOK + 36 * j + 12 * r : 2 * TOK + 36 * j + 12 * r + 12] for j in range(4)]
+            row = [jnp.zeros((6, 512), F32)] + row + [jnp.zeros((10, 512), F32)]
+            yext[48 + r] = jnp.concatenate(row, 0).astype(BF)
+        pole_copy.start()
+
     ret_copy(3, 36, 12).start()
     normed = add_mixed(1, others)
     for n in range(4):
         expand(1, normed, others, n)
-    y = jnp.concatenate([y, contract(1, others)], 0)
+    y = jnp.concatenate([contract(1, others), y[0 : 2 * TOK]], 0)
     for band in range(2):
         for r in range(6):
             row = [y[TOK * w + 12 * r : TOK * w + 12 * r + 12] for w in (ORDER.index((band, j)) for j in range(4))]
@@ -374,23 +395,6 @@
 
     @pl.when(south)
     def _():
-        x = ext[48:51].astype(F32)
-        for w in range(2):
-            wide[TOK * w : TOK * w + TOK] = jnp.concatenate(
-                [x[r, 12 * j + 6 : 12 * j + 18] for j in (2 * w, 2 * w + 1) for r in range(3)], 0
-            )
-            bias[w] = window_bias([vflag[r : r + 1] for r in range(5, 8)], 6 + 24 * w, halves=True)
-        project(1, 2 * TOK)
-        attend(0)
-        normed = add_mixed(1, first)
-        for n in range(4):
-            expand(1, normed, first, n)
-        y = contract(1, first)
-        for r in range(3):
-            row = [y[36 * j + 12 * r : 36 * j + 12 * r + 12] for j in range(4)]
-            row = [jnp.zeros((6, 512), F32)] + row + [jnp.zeros((10, 512), F32)]
-            yext[48 + r] = jnp.concatenate(row, 0).astype(BF)
-        pole_copy.start()
         pole_copy.wait()
 
     @pl.when(~south)
@@ -441,14 +445,17 @@
     return jnp.concatenate(parts, axis=1)
 
 
-def deliver(src, dst, sem):
-    copies = [
-        pltpu.make_async_copy(src.at[pl.ds(6 * n, 6)], dst.at[pl.ds(6 * n, 6)], sem.at[n]) for n in range(8)
-    ]
-    for copy in copies:
-        copy.start()
-    for copy in copies:
-        copy.wait()
+def deliver(src, dst, held, load_sem, store_sem):
+    parts = [pl.ds(6 * n, 6) for n in range(8)]
+    loads = [pltpu.make_async_copy(src.at[part], held.at[part], load_sem.at[n]) for n, part in enumerate(parts)]
+    stores = [pltpu.make_async_copy(held.at[part], dst.at[part], store_sem.at[n]) for n, part in enumerate(parts)]
+    for load in loads:
+        load.start()
+    for load, store in zip(loads, stores):
+        load.wait()
+        store.start()
+    for store in stores:
+        store.wait()
 
 
 def shards(tokens, valid, w_qkv, w_out, w_up, w_down):
@@ -471,12 +478,12 @@
             pltpu.VMEM((2, 512, 512), BF),
             pltpu.VMEM((2, 512, 2048), BF),
             pltpu.VMEM((2, 2048, 512), BF),
-            pltpu.VMEM((8, PAD, 1536), BF),
-            pltpu.VMEM((576, 512), BF),
-            pltpu.VMEM((576, 512), F32),
-            pltpu.VMEM((576, 512), BF),
-            pltpu.VMEM((576, 2048), BF),
-            pltpu.VMEM((8, TOK, 256), F32),
+            pltpu.VMEM((10, PAD, 1536), BF),
+            pltpu.VMEM((720, 512), BF),
+            pltpu.VMEM((720, 512), F32),
+            pltpu.VMEM((720, 512), BF),
+            pltpu.VMEM((720, 2048), BF),
+            pltpu.VMEM((10, TOK, 256), F32),
             dma((4,)), dma((2, 4)), dma((4,)),
             dma((4,)), dma((4,)), dma(()), dma(()), dma(()), dma(()), dma(()), dma(()),
             dma((4,)), dma((4,)), dma(()), dma(()), dma(()), dma(()),
@@ -491,7 +498,7 @@
         out_shape=result,
         in_specs=[hbm],
         out_specs=hbm,
-        scratch_shapes=[dma((8,))],
+        scratch_shapes=[pltpu.VMEM((48, 48, 512), BF), dma((8,)), dma((8,))],
         name="deliver",
     )(done)
 

time: 140 us -> 63.6 us (0.45)
  Pallas kernels: 140 us -> 63.3 us
    pallas_call x1, Pallas kernels: 72.6 us -> 2.49 us  [shards(): pl.pallas_call(deliver, out_shape=result, in_specs=[hbm], out_specs=hbm,...]
    pallas_call x1, Pallas kernels: 67.1 us -> 60.8 us  [shards(): pl.pallas_call(kernel, out_shape=result, in_specs=[hbm, vmem] + [hbm] * 4...]
where the time goes in v3:
time: 63.6 us; the launch traced here: 63.5 us
  Pallas kernels  63.3 us (100%)
    pallas_call x1, Pallas kernels, shards(): pl.pallas_call(kernel, out_shape=result, in_specs=[hbm, vmem] + [hbm] * 4...  60.8 us
    pallas_call x1, Pallas kernels, shards(): pl.pallas_call(deliver, out_shape=result, in_specs=[hbm], out_specs=hbm,...  2.49 us

profile of v3, /device:TPU:28, one launch (start us, length us, event | category | flops | bytes accessed | tf_op | source)
XLA Modules:
  0.0 63.5 jit_solution(11870151572274175998)
XLA Ops:
  0.0 60.8 %swin.1.src = bf16[48,48,512]{2,1,0:T(8,128)(2,1)} custom-call(bf16[48,48,512]{2,1,0:T(8,128)(2,1)} %tok_hbm.1, s32[48,48]{1,0:T(8,128)} %valid_ref.1, bf16[2,512,1536]{2,1,0:T(8,128)(2,1)} %wqkv_hbm.1, bf16[2,512,512]{2,1,0:T(8,128)(2,1)} %wout_hbm.1, bf16[2,512,2048]{2,1,0:T(8,128)(2,1)} %wup_hbm.1, bf16[2,2048,512]{2,1,0:T(8,128)(2,1)} %wdown_hbm.1, ...), custom_call_target="tpu_custom_call" | custom-call | tf_op jit(solution)/shard_map/swin/pallas_call | solution.py:466
  60.8 2.5 %deliver.1 = bf16[48,48,512]{2,1,0:T(8,128)(2,1)} custom-call(bf16[48,48,512]{2,1,0:T(8,128)(2,1)} %swin.1.src), custom_call_target="tpu_custom_call" | custom-call | tf_op jit(solution)/shard_map/deliver/pallas_call | solution.py:496

commit v4 on v3

--- a/solution.py
+++ b/solution.py
@@ -47,7 +47,7 @@
         if bias is not None:
             part = part + bias
         largest = jnp.max(part, axis=0, keepdims=True)
-        expo = jnp.exp2(part - largest)
+        expo = jnp.exp2((part - largest) * SCALE)
         total = jnp.sum(expo, axis=0, keepdims=True)
         parts += [expo * (1.0 / total), jnp.zeros((PAD - TOK, 3 * PAD), F32)]
     probs = jnp.concatenate(parts, 0).astype(BF)
@@ -83,9 +83,9 @@
 def kernel(
     tok_hbm, valid_ref, wqkv_hbm, wout_hbm, wup_hbm, wdown_hbm, sets_ref,
     out_hbm,
-    tok, ext, yext, ret, vhalo, wqkv, wout, wup, wdown, qkv, mixed, wide, resid, hidden, bias,
+    tok, ext, yext, outgoing, ret, edge_out, edge_in, vhalo, wqkv, wout, wup, wdown, qkv, mixed, wide, resid, hidden, bias,
     tok_sem, w_sem, out_sem, halo_s, halo_r, row_s, row_r, diag_s, diag_r, v_s, v_r,
-    ret_s, ret_r, corner_s, corner_r, below_s, below_r,
+    ret_s, ret_r, corner_s, corner_r, pole_s, below_s, below_r,
 ):
     lat, lon = lax.axis_index("lat"), lax.axis_index("lon")
     lats, lons = lax.axis_size("lat"), lax.axis_size("lon")
@@ -119,7 +119,21 @@
         pl.semaphore_signal(barrier, inc=1, device_id=place, device_id_type=MESH)
 
     qkv[:, TOK:PAD, :] = jnp.zeros((10, PAD - TOK, 1536), BF)
-    bias[...] = jnp.zeros((10, TOK, 256), F32)
+    bias[...] = jnp.zeros((26, TOK, 256), F32)
+    one = jnp.ones((1, 128), F32)
+    vflag = flag_rows(valid_ref, None)
+
+    @pl.when(south)
+    def _():
+        for w, (band, j) in enumerate(ORDER):
+            if band == 1:
+                bias[w] = window_bias([vflag[r : r + 1] for r in range(2, 8)], 12 * j)
+
+    @pl.when(north)
+    def _():
+        for w, (band, j) in enumerate(ORDER):
+            if band == 0:
+                bias[8 + w] = window_bias([0.0 * one] * 3 + [one] * 3, 6 + 12 * j)
 
     @pl.when(north)
     def _():
@@ -146,23 +160,16 @@
         ext.at[pl.ds(48, 3), pl.ds(0, HALO)], ext.at[pl.ds(0, 3), pl.ds(48, HALO)], diag_s, diag_r, (lat + 1, left)
     )
 
-    def ret_copy(p, low, size):
-        rows = pl.ds(low, size)
-        return send(yext.at[rows, pl.ds(48, HALO)], ret.at[rows], ret_s.at[p], ret_r.at[p], (lat, right))
-
-    below_copy = send(
-        yext.at[pl.ds(0, 3), pl.ds(0, 48)], yext.at[pl.ds(48, 3), pl.ds(0, 48)], below_s, below_r, (lat - 1, lon)
-    )
-    corner_copy = send(
-        yext.at[pl.ds(0, 3), pl.ds(48, HALO)], ret.at[pl.ds(48, 3)], corner_s, corner_r, (lat - 1, right)
-    )
-    pole_copy = send(
-        yext.at[pl.ds(48, 3), pl.ds(48, HALO)], ret.at[pl.ds(48, 3)], corner_s, corner_r, (lat, right)
-    )
+    def ret_copy(p):
+        return send(outgoing.at[p], ret.at[p], ret_s.at[p], ret_r.at[p], (lat, right))
+
+    below_copy = send(yext.at[pl.ds(0, 3)], yext.at[pl.ds(48, 3)], below_s, below_r, (lat - 1, lon))
+    corner_copy = send(outgoing.at[0, pl.ds(0, 32)], edge_in, corner_s, corner_r, (lat - 1, right))
+    pole_copy = send(edge_out, edge_in, pole_s, corner_r, (lat, right))
 
     def out_copy(n, low, size):
         return pltpu.make_async_copy(
-            yext.at[pl.ds(low, size), pl.ds(0, 48)], out_hbm.at[pl.ds(low - 3, size)], out_sem.at[n]
+            yext.at[pl.ds(low, size)], out_hbm.at[pl.ds(low - 3, size)], out_sem.at[n]
         )
 
     sets = [sets_ref[i] for i in range(6)]
@@ -184,18 +191,16 @@
     def project(b, x, tokens):
         out = jnp.dot(layer_norm(x), wqkv[b], preferred_element_type=F32)
         for w in range(tokens // TOK):
-            rows = slice(TOK * w, TOK * w + TOK)
-            qkv[w, 0:TOK, 0:512] = (out[rows, 0:512] * SCALE).astype(BF)
-            qkv[w, 0:TOK, 512:1536] = out[rows, 512:1536].astype(BF)
-
-    def attend(pair, masked):
+            qkv[w, 0:TOK, :] = out[TOK * w : TOK * w + TOK].astype(BF)
+
+    def attend(pair, flagged):
         for g in range(2):
             both = []
             for w in (2 * pair, 2 * pair + 1):
                 q = qkv[w, :, 256 * g : 256 * g + 256]
                 k = qkv[w, :, 512 + 256 * g : 768 + 256 * g]
                 v = qkv[w, :, 1024 + 256 * g : 1280 + 256 * g]
-                both.append(half_heads(q, k, v, sets, bias[w, :, 0 : 3 * PAD] if masked else None))
+                both.append(half_heads(q, k, v, sets, None if flagged is None else bias[flagged + w, :, 0 : 3 * PAD]))
             mixed[2 * TOK * pair : 2 * TOK * pair + 2 * TOK, 256 * g : 256 * g + 256] = jnp.concatenate(
                 both, 0
             ).astype(BF)
@@ -222,46 +227,40 @@
         ]
         ext[pl.ds(3 + 12 * p, 12), 0:48] = jnp.concatenate(rows, 0).astype(BF).reshape(12, 48, 512)
 
-    def scatter1(y, p):
+    def pack(y, p):
+        part = [y[TOK * band + 12 * r + 6 : TOK * band + 12 * r + 12] for band in range(2) for r in range(6)]
+        outgoing[p] = jnp.concatenate(part + [jnp.zeros((PAD - TOK, 512), F32)], 0).astype(BF)
+
+    def settle(y, p):
         for band in range(2):
             for r in range(6):
                 row = [y[TOK * w + 12 * r : TOK * w + 12 * r + 12] for w in (ORDER.index((band, j)) for j in range(4))]
-                row = [jnp.zeros((6, 512), F32)] + row + [jnp.zeros((10, 512), F32)]
-                yext[12 * p + 6 * band + r] = jnp.concatenate(row, 0).astype(BF)
+                row = [jnp.zeros((6, 512), F32)] + row
+                yext[12 * p + 6 * band + r] = jnp.concatenate(row, 0)[0:48].astype(BF)
+
+    def scatter1(y, p):
+        pack(y[6 * TOK : 8 * TOK], p)
+        settle(y, p)
 
     everything = slice(0, 576)
 
-    def step(b_feed, p_feed, b_att, gather, p_att, scatter, masked=False, edge=False):
+    def step(b_feed, p_feed, b_att, gather, p_att, scatter, flagged=None, edge=False):
         normed = add_mixed(b_feed, everything)
         gather(p_att)
         project(b_att, wide[0:720] if edge else wide[0:576], 720 if edge else 576)
         for n in range(4):
             expand(b_feed, normed, everything, n)
-            attend(n, masked)
+            attend(n, flagged)
         if edge:
-            attend(4, masked)
+            attend(4, flagged)
         scatter(contract(b_feed, everything), p_feed)
-
-    vflag = flag_rows(valid_ref, None)
-
-    @pl.when(south)
-    def _():
-        for w, (band, j) in enumerate(ORDER):
-            if band == 1:
-                bias[w] = window_bias([vflag[r : r + 1] for r in range(2, 8)], 12 * j)
 
     tok_copy(3).wait()
     weights[0][0].wait()
     gather0(3)
     project(0, wide[0:576], 576)
     for n in range(4):
-        attend(n, True)
-
-    @pl.when(south)
-    def _():
-        for w, (band, j) in enumerate(ORDER):
-            if band == 1:
-                bias[w] = jnp.zeros((TOK, 256), F32)
+        attend(n, 0)
 
     for n in range(1, 4):
         weights[0][n].wait()
@@ -285,15 +284,16 @@
 
     v_copy.wait()
     vflag = flag_rows(valid_ref, vhalo)
-    one = jnp.ones((1, 128), F32)
     for n in range(4):
         weights[1][n].wait()
 
-    @pl.when(north)
+    @pl.when(south)
     def _():
         for w, (band, j) in enumerate(ORDER):
-            if band == 0:
-                bias[w] = window_bias([0.0 * one] * 3 + [one] * 3, 6 + 12 * j)
+            if band == 1:
+                bias[16 + w] = window_bias([one] + [vflag[r : r + 1] for r in range(5)], 6 + 12 * j)
+        for w in range(2):
+            bias[24 + w] = window_bias([vflag[r : r + 1] for r in range(5, 8)], 6 + 24 * w, halves=True)
 
     @pl.when(~north)
     def _():
@@ -302,21 +302,14 @@
 
     halo_copy(3).wait_recv()
     halo_copy(0).wait_recv()
-    step(0, 2, 1, gather1, 0, scatter0, masked=True)
+    step(0, 2, 1, gather1, 0, scatter0, flagged=8)
     halo_copy(2).start()
 
-    @pl.when(north)
-    def _():
-        for w, (band, j) in enumerate(ORDER):
-            if band == 0:
-                bias[w] = jnp.zeros((TOK, 256), F32)
-
-    def merge(low, size):
-        rows = pl.ds(low, size)
-        col = lax.broadcasted_iota(jnp.int32, (1, HALO, 512), 1)
-        yext[rows, 0:HALO] = jnp.where(
-            col < 6, ret[rows].astype(F32), yext[rows, 0:HALO].astype(F32)
-        ).astype(BF)
+    def merge(low, count, source):
+        came = source.astype(F32)
+        for r in range(count):
+            own = yext[low + r, 0:HALO].astype(F32)
+            yext[low + r, 0:HALO] = jnp.concatenate([came[6 * r : 6 * r + 6], own[6:]], 0).astype(BF)
 
     def block1(p, carry):
         halo_copy(p).wait_recv()
@@ -324,7 +317,7 @@
 
         @pl.when(p == 1)
         def _():
-            ret_copy(0, 3, 9).start()
+            ret_copy(0).start()
 
             @pl.when(~north)
             def _():
@@ -333,23 +326,14 @@
 
         @pl.when(p == 2)
         def _():
-            ret_copy(1, 12, 12).start()
-            ret_copy(0, 3, 9).wait_recv()
-            merge(3, 9)
+            ret_copy(1).start()
+            ret_copy(0).wait_recv()
+            merge(3, 9, ret[0, 18:72])
             out_copy(0, 3, 9).start()
 
         return carry
 
     lax.fori_loop(1, 3, block1, 0)
-
-    @pl.when(south)
-    def _():
-        for w, (band, j) in enumerate(ORDER):
-            if band == 1:
-                bias[w] = window_bias([one] + [vflag[r : r + 1] for r in range(5)], 6 + 12 * j)
-
-    for w in range(2):
-        bias[8 + w] = window_bias([vflag[r : r + 1] for r in range(5, 8)], 6 + 24 * w, halves=True)
 
     def gather_last(p):
         gather1(p)
@@ -358,10 +342,10 @@
             [x[r, 12 * j + 6 : 12 * j + 18] for j in range(4) for r in range(3)], 0
         )
 
-    step(1, 2, 1, gather_last, 3, scatter1, masked=True, edge=True)
-    ret_copy(2, 24, 12).start()
-    ret_copy(1, 12, 12).wait_recv()
-    merge(12, 12)
+    step(1, 2, 1, gather_last, 3, scatter1, flagged=16, edge=True)
+    ret_copy(2).start()
+    ret_copy(1).wait_recv()
+    merge(12, 12, ret[1])
     out_copy(1, 12, 12).start()
 
     others, first = slice(0, 6 * TOK), slice(6 * TOK, 10 * TOK)
@@ -369,29 +353,22 @@
     for n in range(4):
         expand(1, normed, first, n)
     y = contract(1, first)
-    for band in range(2):
-        for r in range(6):
-            row = [y[TOK * band + 12 * r + 6 : TOK * band + 12 * r + 12], jnp.zeros((10, 512), F32)]
-            yext[36 + 6 * band + r, 48:64] = jnp.concatenate(row, 0).astype(BF)
+    pack(y[0 : 2 * TOK], 3)
 
     @pl.when(south)
     def _():
+        part = [y[2 * TOK + 108 + 12 * r + 6 : 2 * TOK + 108 + 12 * r + 12] for r in range(3)]
+        edge_out[...] = jnp.concatenate(part + [jnp.zeros((14, 512), F32)], 0).astype(BF)
+        pole_copy.start()
         for r in range(3):
             row = [y[2 * TOK + 36 * j + 12 * r : 2 * TOK + 36 * j + 12 * r + 12] for j in range(4)]
-            row = [jnp.zeros((6, 512), F32)] + row + [jnp.zeros((10, 512), F32)]
-            yext[48 + r] = jnp.concatenate(row, 0).astype(BF)
-        pole_copy.start()
-
-    ret_copy(3, 36, 12).start()
+            yext[48 + r] = jnp.concatenate([jnp.zeros((6, 512), F32)] + row, 0)[0:48].astype(BF)
+
+    ret_copy(3).start()
     normed = add_mixed(1, others)
     for n in range(4):
         expand(1, normed, others, n)
-    y = jnp.concatenate([contract(1, others), y[0 : 2 * TOK]], 0)
-    for band in range(2):
-        for r in range(6):
-            row = [y[TOK * w + 12 * r : TOK * w + 12 * r + 12] for w in (ORDER.index((band, j)) for j in range(4))]
-            row = [jnp.zeros((6, 512), F32)] + row
-            yext[36 + 6 * band + r, 0:48] = jnp.concatenate(row, 0)[0:48].astype(BF)
+    settle(jnp.concatenate([contract(1, others), y[0 : 2 * TOK]], 0), 3)
 
     @pl.when(south)
     def _():
@@ -402,23 +379,22 @@
         below_copy.wait_recv()
         corner_copy.wait_recv()
 
-    ret_copy(2, 24, 12).wait_recv()
-    merge(24, 12)
+    ret_copy(2).wait_recv()
+    merge(24, 12, ret[2])
     out_copy(2, 24, 12).start()
-    ret_copy(3, 36, 12).wait_recv()
-    merge(36, 15)
+    ret_copy(3).wait_recv()
+    merge(36, 12, ret[3])
+    merge(48, 3, edge_in[...])
     lane = lax.broadcasted_iota(jnp.int32, (48, 128), 1)
     sub = lax.broadcasted_iota(jnp.int32, (48, 128), 0)
     for r in range(8):
         keep = jnp.sum(jnp.where(lane == sub, vflag[r : r + 1], 0.0), axis=1, keepdims=True)
-        yext[43 + r, 0:48] = (yext[43 + r, 0:48].astype(F32) * keep).astype(BF)
+        yext[43 + r] = (yext[43 + r].astype(F32) * keep).astype(BF)
     out_copy(3, 36, 15).start()
 
     for p in range(4):
         halo_copy(p).wait_send()
-    ret_copy(0, 3, 9).wait_send()
-    for p in range(1, 4):
-        ret_copy(p, 12 * p, 12).wait_send()
+        ret_copy(p).wait_send()
 
     @pl.when(~south)
     def _():
@@ -471,8 +447,11 @@
         scratch_shapes=[
             pltpu.VMEM((48, 48, 512), BF),
             pltpu.VMEM((51, EXT, 512), BF),
-            pltpu.VMEM((51, EXT, 512), BF),
-            pltpu.VMEM((51, HALO, 512), BF),
+            pltpu.VMEM((51, 48, 512), BF),
+            pltpu.VMEM((4, PAD, 512), BF),
+            pltpu.VMEM((4, PAD, 512), BF),
+            pltpu.VMEM((32, 512), BF),
+            pltpu.VMEM((32, 512), BF),
             pltpu.VMEM((8, 48), jnp.int32),
             pltpu.VMEM((2, 512, 1536), BF),
             pltpu.VMEM((2, 512, 512), BF),
@@ -483,10 +462,10 @@
             pltpu.VMEM((720, 512), F32),
             pltpu.VMEM((720, 512), BF),
             pltpu.VMEM((720, 2048), BF),
-            pltpu.VMEM((10, TOK, 256), F32),
+            pltpu.VMEM((26, TOK, 256), F32),
             dma((4,)), dma((2, 4)), dma((4,)),
             dma((4,)), dma((4,)), dma(()), dma(()), dma(()), dma(()), dma(()), dma(()),
-            dma((4,)), dma((4,)), dma(()), dma(()), dma(()), dma(()),
+            dma((4,)), dma((4,)), dma(()), dma(()), dma(()), dma(()), dma(()),
         ],
         compiler_params=pltpu.CompilerParams(
             collective_id=0, has_side_effects=True, vmem_limit_bytes=60 << 20

time: 63.6 us -> 63.8 us (level)
  no operation moved by 1% of the time
where the time goes in v4:
time: 63.8 us; the launch traced here: 63.6 us
  Pallas kernels  63.4 us (99%)
    pallas_call x1, Pallas kernels, shards(): pl.pallas_call(kernel, out_shape=result, in_specs=[hbm, vmem] + [hbm] * 4...  60.9 us
    pallas_call x1, Pallas kernels, shards(): pl.pallas_call(deliver, out_shape=result, in_specs=[hbm], out_specs=hbm,...  2.49 us

profile of v4, /device:TPU:28, one launch (start us, length us, event | category | flops | bytes accessed | tf_op | source)
XLA Modules:
  0.0 63.6 jit_solution(10245263907623106108)
XLA Ops:
  0.0 60.9 %swin.1.src = bf16[48,48,512]{2,1,0:T(8,128)(2,1)} custom-call(bf16[48,48,512]{2,1,0:T(8,128)(2,1)} %tok_hbm.1, s32[48,48]{1,0:T(8,128)} %valid_ref.1, bf16[2,512,1536]{2,1,0:T(8,128)(2,1)} %wqkv_hbm.1, bf16[2,512,512]{2,1,0:T(8,128)(2,1)} %wout_hbm.1, bf16[2,512,2048]{2,1,0:T(8,128)(2,1)} %wup_hbm.1, bf16[2,2048,512]{2,1,0:T(8,128)(2,1)} %wdown_hbm.1, ...), custom_call_target="tpu_custom_call" | custom-call | tf_op jit(solution)/shard_map/swin/pallas_call | solution.py:442
  60.9 2.5 %deliver.1 = bf16[48,48,512]{2,1,0:T(8,128)(2,1)} custom-call(bf16[48,48,512]{2,1,0:T(8,128)(2,1)} %swin.1.src), custom_call_target="tpu_custom_call" | custom-call | tf_op jit(solution)/shard_map/deliver/pallas_call | solution.py:475
